TPU v7x, 512 devices: a whole 4x8x8 slice. The times are simulated.
512 devices in a mesh: dp: 128 (over y, z, core), seq: 4 (over x).
Axes of the slice: x: 4, y: 8, z: 8, core: 2. Of those that a mesh axis runs over, the one named last changes fastest.
Arguments:
- residual: bfloat16 [131072, 2048], P(('dp', 'seq')), may hold values from -6 to 6
- queries: bfloat16 [32768, 2048], P(('dp', 'seq'))
- key_proj: bfloat16 [32768, 2048], P(('dp', 'seq'))
- value_proj: bfloat16 [32768, 2048], P(('dp', 'seq')), may hold values from -6 to 6
- out_grad: bfloat16 [32768, 2048], P(('dp', 'seq')), may hold values from -6 to 6
- router: float32 [2048], replicated, may hold values from -0.125 to 0.125
- counts: int32 [128, 4], replicated, may hold values from 1 to 63, as said below
- kept_rows: int32 [128, 4, 64], replicated, may hold values from 0 to 255, as said below
Outputs:
- block_out: bfloat16 [131072, 2048], P(('dp', 'seq'))
- query_grad: bfloat16 [32768, 2048], P(('dp', 'seq'))
- key_grad: bfloat16 [32768, 2048], P(('dp', 'seq'))
- value_grad: bfloat16 [32768, 2048], P(('dp', 'seq'))
- router_grad: float32 [2048], replicated
Inputs may be any that keep to these rules, and one draw needn't show every extreme that they name: Device block (n, b) and block (n + 128 / 2 mod 128, b) have counts that add up to 64. `kept_rows`: for each sequence and block the first counts[n, b] entries are distinct and rising; the other entries are 0.
All inputs are finite; a program needn't handle non-finite values.
Results may differ from a plain program's by a relative error of at most 0.0058.
Values may be sent and summed in bfloat16 or wider, within the bound.
No kernel may reach another device: no remote copies, remote signals or barrier semaphores. Data moves between devices by JAX's collectives and lax.ppermute only.
A program may use at most 64 MiB of HBM per device.

v0:
```python
import math

import jax
import jax.numpy as jnp
from jax import lax
from jax.sharding import PartitionSpec as P

HEADS = 16


def swapped(value, axis, distance):
    mask = 2**distance
    pairs = [(source, source ^ mask) for source in range(lax.axis_size(axis))]
    return lax.ppermute(value, axis, pairs)


def attend_rows(
    q_rows, k_rows, v_rows, x_rows, g_rows, router, q_pos, q_tag, q_live, k_pos, k_tag, k_live
):
    width = q_rows.shape[1]
    head_dim = width // HEADS
    inv_scale = 1.0 / math.sqrt(head_dim)
    qh = q_rows.reshape(-1, HEADS, head_dim)
    kh = k_rows.reshape(-1, HEADS, head_dim)
    vh = v_rows.reshape(-1, HEADS, head_dim)
    scores = jnp.einsum("qhd,khd->hqk", qh, kh, preferred_element_type=jnp.float32) * inv_scale
    allowed = (
        k_live[None, :] & (k_tag[None, :] == q_tag[:, None]) & (k_pos[None, :] <= q_pos[:, None])
    )
    scores = jnp.where(allowed[None], scores, -1e30)
    probs = jax.nn.softmax(scores, axis=-1)
    probs_low = probs.astype(jnp.bfloat16)
    attended = jnp.einsum(
        "hqk,khd->qhd", probs_low, vh, preferred_element_type=jnp.float32
    ).reshape(-1, width)
    x_wide = x_rows.astype(jnp.float32)
    gate = jax.nn.sigmoid(jnp.dot(x_wide, router, precision=lax.Precision.HIGHEST))
    mixed = x_wide + gate[:, None] * attended
    live_f = q_live.astype(jnp.float32)
    g_wide = g_rows.astype(jnp.float32)
    d_att = ((gate * live_f)[:, None] * g_wide).astype(jnp.bfloat16)
    d_gate = jnp.sum(g_wide * attended, axis=-1)
    d_logit = d_gate * gate * (1.0 - gate) * live_f
    d_router = jnp.dot(d_logit, x_wide, precision=lax.Precision.HIGHEST)
    dah = d_att.reshape(-1, HEADS, head_dim)
    d_probs = jnp.einsum("qhd,khd->hqk", dah, vh, preferred_element_type=jnp.float32)
    d_scores = probs * (d_probs - jnp.sum(probs * d_probs, axis=-1, keepdims=True)) * inv_scale
    d_scores = d_scores.astype(jnp.bfloat16)
    d_query = jnp.einsum("hqk,khd->qhd", d_scores, kh, preferred_element_type=jnp.float32).reshape(
        -1, width
    )
    d_key = jnp.einsum("hqk,qhd->khd", d_scores, qh, preferred_element_type=jnp.float32).reshape(
        -1, width
    )
    d_value = jnp.einsum(
        "hqk,qhd->khd", probs_low, dah, preferred_element_type=jnp.float32
    ).reshape(-1, width)
    return (mixed, d_query, d_key, d_value, d_router)


def shards(residual, queries, key_proj, value_proj, out_grad, router, counts, kept_rows):
    dp_index = lax.axis_index("dp")
    seq_index = lax.axis_index("seq")
    dp_count = lax.axis_size("dp")
    seq_count = lax.axis_size("seq")
    tok_dev = residual.shape[0]
    capacity = kept_rows.shape[2]
    mean_kept = capacity // 2
    slot_ids = jnp.arange(capacity, dtype=jnp.int32)
    group_counts = counts[dp_index]
    group_rows = kept_rows[dp_index]
    own_count = group_counts[seq_index]
    own_rows = group_rows[seq_index]
    own_live = slot_ids < own_count
    x_own = jnp.take(residual, own_rows, axis=0)
    gathered_keys, gathered_values = (
        lax.all_gather(key_proj, "seq", axis=0, tiled=True),
        lax.all_gather(value_proj, "seq", axis=0, tiled=True),
    )
    base_pos = seq_index * tok_dev
    n_keys = seq_count * capacity

    def key_layout(block_counts, block_rows):
        key_pos = (jnp.arange(seq_count, dtype=jnp.int32)[:, None] * tok_dev + block_rows).reshape(
            -1
        )
        key_live = (slot_ids[None, :] < block_counts[:, None]).reshape(-1)
        return (key_pos, key_live)

    home_pos, home_live = key_layout(group_counts, group_rows)
    half_dp = dp_count // 2
    top_bit = half_dp.bit_length() - 1
    partner = (dp_index + half_dp) % dp_count
    partner_counts = counts[partner]
    partner_rows = kept_rows[partner]
    far_q, far_x, far_g, far_keys, far_values = swapped(
        (
            queries[mean_kept:],
            x_own[mean_kept:],
            out_grad[mean_kept:],
            gathered_keys,
            gathered_values,
        ),
        "dp",
        top_bit,
    )
    own_keep = jnp.minimum(own_count, mean_kept)
    far_count = jnp.maximum(partner_counts[seq_index] - mean_kept, 0)
    packed_ids = jnp.arange(mean_kept, dtype=jnp.int32)
    is_home = packed_ids < own_keep
    far_slot = jnp.clip(packed_ids - own_keep, 0, mean_kept - 1)

    def pack(home_rows, away_rows):
        return jnp.where(
            is_home[:, None], home_rows[:mean_kept], jnp.take(away_rows, far_slot, axis=0)
        )

    q_pos = base_pos + jnp.where(
        is_home, own_rows[:mean_kept], partner_rows[seq_index][mean_kept + far_slot]
    )
    q_live = is_home | (packed_ids - own_keep < far_count)
    q_tag = jnp.where(is_home, 0, 1).astype(jnp.int32)
    far_pos, far_live = key_layout(partner_counts, partner_rows)
    all_keys = jnp.concatenate([gathered_keys, far_keys], axis=0)
    all_values = jnp.concatenate([gathered_values, far_values], axis=0)
    k_pos = jnp.concatenate([home_pos, far_pos])
    k_live = jnp.concatenate([home_live, far_live])
    k_tag = jnp.concatenate([jnp.zeros((n_keys,), jnp.int32), jnp.ones((n_keys,), jnp.int32)])
    mixed, d_query, d_key, d_value, d_router = attend_rows(
        pack(queries, far_q),
        all_keys,
        all_values,
        pack(x_own, far_x),
        pack(out_grad, far_g),
        router,
        q_pos,
        q_tag,
        q_live,
        k_pos,
        k_tag,
        k_live,
    )
    back_slot = jnp.clip(own_keep + packed_ids, 0, mean_kept - 1)
    back_mixed, back_query, back_key, back_value = swapped(
        (
            jnp.take(mixed, back_slot, axis=0),
            jnp.take(d_query, back_slot, axis=0),
            d_key[n_keys:],
            d_value[n_keys:],
        ),
        "dp",
        top_bit,
    )
    mixed_list = jnp.concatenate([mixed, back_mixed], axis=0)
    query_list = jnp.concatenate([d_query, back_query], axis=0)
    key_terms = d_key[:n_keys] + back_key
    value_terms = d_value[:n_keys] + back_value
    key_sum, value_sum = (
        lax.psum_scatter(key_terms, "seq", scatter_dimension=0, tiled=True),
        lax.psum_scatter(value_terms, "seq", scatter_dimension=0, tiled=True),
    )
    router_total = lax.psum(d_router, ("dp", "seq"))
    target = jnp.where(own_live, own_rows, tok_dev)
    block_out = residual.at[target].set(mixed_list.astype(jnp.bfloat16), mode="drop")
    live_col = own_live[:, None]
    query_grad = jnp.where(live_col, query_list, 0.0).astype(jnp.bfloat16)
    key_grad = jnp.where(live_col, key_sum, 0.0).astype(jnp.bfloat16)
    value_grad = jnp.where(live_col, value_sum, 0.0).astype(jnp.bfloat16)
    return (block_out, query_grad, key_grad, value_grad, router_total)


def solution(mesh):
    return jax.shard_map(
        shards,
        mesh=mesh,
        in_specs=(
            P(("dp", "seq"), None),
            P(("dp", "seq"), None),
            P(("dp", "seq"), None),
            P(("dp", "seq"), None),
            P(("dp", "seq"), None),
            P(),
            P(),
            P(),
        ),
        out_specs=(
            P(("dp", "seq"), None),
            P(("dp", "seq"), None),
            P(("dp", "seq"), None),
            P(("dp", "seq"), None),
            P(),
        ),
        check_vma=False,
    )
```

profile of v0, /device:TPU:1, one launch (start us, length us, event | category | flops | bytes accessed | tf_op | source)
XLA Modules:
  0.0 486.4 jit_solution(2525668509017830493)
XLA Ops:
  7.3 1.3 copy.85
  8.6 8.3 %collective-permute-start.5 = (bf16[32,2048]{1,0:T(8,128)(2,1)S(1)}, bf16[32,2048]{1,0:T(8,128)(2,1)S(1)}, u32[]{:S(2)}, u32[]{:S(2)}) collective-permute-start(bf16[32,2048]{1,0:T(8,128)(2,1)S(1)} %slice.55), channel_id=1, source_target_pairs={{0,256},{4,260},{8,264},{12,268},{16,272},{20,276},{24,280},{28,28... | collective-permute-start | bytes 393224 | tf_op jit(solution)/shard_map/ppermute | solution.py:14
  17.0 1.9 collective-permute-start.2
  18.9 0.6 fusion.60
  19.5 0.2 dynamic-slice_reduce_fusion.2
  19.7 1.1 fusion.41
  20.8 0.7 gather_fusion
  21.6 0.1 broadcast_select_fusion
  21.7 7.3 %collective-permute-start = (bf16[32,2048]{1,0:T(8,128)(2,1)S(1)}, bf16[32,2048]{1,0:T(8,128)(2,1)S(1)}, u32[]{:S(2)}, u32[]{:S(2)}) collective-permute-start(bf16[32,2048]{1,0:T(8,128)(2,1)S(1)} %slice.79), channel_id=1, source_target_pairs={{0,256},{4,260},{8,264},{12,268},{16,272},{20,276},{24,280},{28,28... | collective-permute-start | bytes 393224 | tf_op jit(solution)/shard_map/ppermute | solution.py:14
  29.1 0.2 dynamic-slice_reduce_fusion.6
  29.3 0.3 dynamic-slice_reduce_fusion.1
  30.8 0.7 gather_fusion.1
  31.5 0.2 dynamic-slice_reduce_fusion.4
  31.7 12.3 %all-gather.5.cloned.1.call-done = bf16[256,2048]{1,0:T(8,128)(2,1)} async-done(((bf16[64,2048]{1,0:T(8,128)(2,1)}), bf16[256,2048]{1,0:T(8,128)(2,1)}) %all-gather.5.cloned.1.call-update) | async-done | bytes 1048592 | tf_op jit(solution)/shard_map/all_gather | solution.py:77
  44.1 1.5 copy.40
  45.6 7.1 %collective-permute-start.3 = (bf16[256,2048]{0,1:T(8,128)(2,1)S(1)}, bf16[256,2048]{0,1:T(8,128)(2,1)}, u32[]{:S(2)}, u32[]{:S(2)}) collective-permute-start(bf16[256,2048]{0,1:T(8,128)(2,1)S(1)} %copy.40), channel_id=1, source_target_pairs={{0,256},{4,260},{8,264},{12,268},{16,272},{20,276},{24,280},{28,28... | collective-permute-start | bytes 3145736 | tf_op jit(solution)/shard_map/ppermute | solution.py:14
  52.7 0.7 compare_and_fusion
  54.1 1.3 gather_fusion.5
  55.4 0.6 gather_fusion.3
  56.0 0.7 gather_fusion.2
  56.7 0.1 fusion.36
  56.9 19.3 %all-gather.3.cloned.1.call-done = bf16[256,2048]{1,0:T(8,128)(2,1)} async-done(((bf16[64,2048]{1,0:T(8,128)(2,1)}), bf16[256,2048]{1,0:T(8,128)(2,1)}) %all-gather.3.cloned.1.call-update) | async-done | bytes 1048592 | tf_op jit(solution)/shard_map/all_gather | solution.py:78
  76.1 1.5 copy.38
  77.6 7.1 %collective-permute-start.1 = (bf16[256,2048]{0,1:T(8,128)(2,1)S(1)}, bf16[256,2048]{0,1:T(8,128)(2,1)S(1)}, u32[]{:S(2)}, u32[]{:S(2)}) collective-permute-start(bf16[256,2048]{0,1:T(8,128)(2,1)S(1)} %copy.38), channel_id=1, source_target_pairs={{0,256},{4,260},{8,264},{12,268},{16,272},{20,276},{24,280},{28,28... | collective-permute-start | bytes 3145736 | tf_op jit(solution)/shard_map/ppermute | solution.py:14
  84.7 0.8 broadcast_select_fusion.3
  85.6 1.4 collective-permute-done.3
  86.9 1.4 pad_maximum_fusion.1
  88.4 0.4 fusion.7
  88.8 1.2 fusion.62
  90.0 0.4 copy-done.4
  90.4 43.1 %collective-permute-done.1 = bf16[256,2048]{0,1:T(8,128)(2,1)S(1)} collective-permute-done((bf16[256,2048]{0,1:T(8,128)(2,1)S(1)}, bf16[256,2048]{0,1:T(8,128)(2,1)S(1)}, u32[]{:S(2)}, u32[]{:S(2)}) %collective-permute-start.1) | collective-permute-done | bytes 1048608 | tf_op jit(solution)/shard_map/ppermute | solution.py:14
  133.5 0.2 pad_maximum_fusion
  133.7 2.5 convolution_bitcast_fusion.3
  136.3 1.8 fusion.22
  138.1 1.4 fusion.32
  139.5 6.8 %convolution_bitcast_fusion.1 = f32[512,16,128]{0,2,1:T(8,128)} fusion(f32[16,32,512]{2,1,0:T(8,128)} %fusion.32, bf16[4,16,8,128]{3,2,1,0:T(8,128)(2,1)} %copy-done.10, f32[16,32,512]{2,1,0:T(8,128)} %get-tuple-element.33, f32[16,32]{1,0:T(8,128)S(1)} %get-tuple-element.32), kind=kOutput, calls=%fused_computation.11 | convolution fusion | flops 68944896 | bytes 6424576 | tf_op jit(solution)/shard_map/hqk,qhd->khd/dot_general | solution.py:52
  146.3 4.0 fusion.59
  150.3 1.8 copy.50
  152.1 7.8 %collective-permute-start.7 = (f32[256,2048]{1,0:T(8,128)}, f32[256,2048]{1,0:T(8,128)}, u32[]{:S(2)}, u32[]{:S(2)}) collective-permute-start(f32[256,2048]{1,0:T(8,128)} %copy.50), channel_id=1, source_target_pairs={{0,256},{4,260},{8,264},{12,268},{16,272},{20,276},{24,280},{28,28... | collective-permute-start | bytes 6291464 | tf_op jit(solution)/shard_map/ppermute | solution.py:14
  159.9 1.9 copy.51
  161.9 33.7 %collective-permute-done.7 = f32[256,2048]{1,0:T(8,128)} collective-permute-done((f32[256,2048]{1,0:T(8,128)}, f32[256,2048]{1,0:T(8,128)}, u32[]{:S(2)}, u32[]{:S(2)}) %collective-permute-start.7) | collective-permute-done | bytes 2097184 | tf_op jit(solution)/shard_map/ppermute | solution.py:14
  195.5 3.4 add.176
  198.9 4.8 convolution_bitcast_fusion
  203.7 4.0 fusion.58
  207.7 1.9 copy.53
  209.6 7.1 %collective-permute-start.8 = (f32[256,2048]{1,0:T(8,128)}, f32[256,2048]{1,0:T(8,128)}, u32[]{:S(2)}, u32[]{:S(2)}) collective-permute-start(f32[256,2048]{1,0:T(8,128)} %copy.53), channel_id=1, source_target_pairs={{0,256},{4,260},{8,264},{12,268},{16,272},{20,276},{24,280},{28,28... | collective-permute-start | bytes 6291464 | tf_op jit(solution)/shard_map/ppermute | solution.py:14
  216.6 1.9 copy.54
  218.6 65.2 %collective-permute-done.8 = f32[256,2048]{1,0:T(8,128)} collective-permute-done((f32[256,2048]{1,0:T(8,128)}, f32[256,2048]{1,0:T(8,128)}, u32[]{:S(2)}, u32[]{:S(2)}) %collective-permute-start.8) | collective-permute-done | bytes 2097184 | tf_op jit(solution)/shard_map/ppermute | solution.py:14
  283.8 3.4 add.177
  287.2 0.5 compare_and_fusion.1
  287.7 1.2 iota_compare_fusion.2
  288.9 0.6 pad_clamp_fusion
  289.5 5.2 %convolution_bitcast_fusion.2 = bf16[16,4,8,128]{3,2,1,0:T(8,128)(2,1)} fusion(bf16[512,16,128]{0,2,1:T(8,128)(2,1)S(1)} %bitcast.81, f32[16,32,512]{2,1,0:T(8,128)} %fusion.32, f32[16,32,512]{2,1,0:T(8,128)} %get-tuple-element.33, f32[16,32]{1,0:T(8,128)S(1)} %get-tuple-element.32), kind=kOutput, calls=%fused_computation.22 | convolution fusion | flops 68944896 | bytes 4327424 | tf_op jit(solution)/shard_map/hqk,khd->qhd/dot_general | solution.py:49
  294.8 0.9 copy.82
  295.7 0.8 gather_fusion.6
  296.5 0.8 fusion.23
  297.3 0.8 gather_fusion.4
  298.1 0.1 broadcast_select_fusion.1
  298.2 1.9 collective-permute-start.6
  300.1 7.3 %collective-permute-start.4 = (bf16[32,2048]{1,0:T(8,128)(2,1)S(1)}, bf16[32,2048]{1,0:T(8,128)(2,1)S(1)}, u32[]{:S(2)}, u32[]{:S(2)}) collective-permute-start(bf16[32,2048]{1,0:T(8,128)(2,1)S(1)} %get-tuple-element.29), channel_id=1, source_target_pairs={{0,256},{4,260},{8,264},{12,268},{16,272},{20,276},{24,280},{28,28... | collective-permute-start | bytes 393224 | tf_op jit(solution)/shard_map/ppermute | solution.py:14
  307.4 0.2 fusion.43
  307.6 167.9 %psum.7 = f32[2048]{0:T(1024)} all-reduce(f32[2048]{0:T(1024)S(1)} %bitcast.88), channel_id=1, replica_groups=mesh['dp'=128,'seq'=4] {'dp','seq'}, use_global_device_ids=true, to_apply=%region_7.10 | all-reduce | flops 2048 | bytes 16384 | tf_op jit(solution)/shard_map/psum | solution.py:162
  475.6 1.7 scatter_custom_fusion
  477.4 2.5 select_convert_fusion
  (81 shorter events, 1.1 us)
Async XLA Ops:
  7.2 77.6 %copy-start = (f32[2048]{0:T(1024)S(1)}, f32[2048]{0:T(1024)}, u32[]{:S(2)}) copy-start(f32[2048]{0:T(1024)} %param.17) | copy-start | bytes 24580
  7.2 9.8 %copy-start.12 = (bf16[64,2048]{1,0:T(8,128)(2,1)S(1)}, bf16[64,2048]{1,0:T(8,128)(2,1)}, u32[]{:S(2)}) copy-start(bf16[64,2048]{1,0:T(8,128)(2,1)} %param.13) | copy-start | bytes 786436
  7.2 1.4 copy-start.11
  7.2 11.7 %copy-start.14 = (s32[128,4]{0,1:T(4,128)S(1)}, s32[128,4]{0,1:T(4,128)}, u32[]{:S(2)}) copy-start(s32[128,4]{0,1:T(4,128)} %param.18) | copy-start | bytes 6148
  7.2 12.3 %copy-start.9 = (s32[128,4,64]{0,2,1:T(8,128)S(1)}, s32[128,4,64]{0,2,1:T(8,128)}, u32[]{:S(2)}) copy-start(s32[128,4,64]{0,2,1:T(8,128)} %param.19) | copy-start | bytes 393220
  7.2 36.9 %all-gather.5.cloned.1.call-start = ((), (), s32[]{:S(2)}) async-start(), calls=%async_computation.3 | async-start | bytes 1310720 | tf_op jit(solution)/shard_map/all_gather | solution.py:77
  8.6 67.6 %all-gather.3.cloned.1.call-start = ((), (), s32[]{:S(2)}) async-start(), calls=%async_computation.2 | async-start | bytes 1310720 | tf_op jit(solution)/shard_map/all_gather | solution.py:78
  8.6 45.4 %collective-permute-start.5 = (bf16[32,2048]{1,0:T(8,128)(2,1)S(1)}, bf16[32,2048]{1,0:T(8,128)(2,1)S(1)}, u32[]{:S(2)}, u32[]{:S(2)}) collective-permute-start(bf16[32,2048]{1,0:T(8,128)(2,1)S(1)} %slice.55), channel_id=1, source_target_pairs={{0,256},{4,260},{8,264},{12,268},{16,272},{20,276},{24,280},{28,28... | collective-permute-start | bytes 393224 | tf_op jit(solution)/shard_map/ppermute | solution.py:14
  17.0 38.4 %collective-permute-start.2 = (bf16[32,2048]{1,0:T(8,128)(2,1)S(1)}, bf16[32,2048]{1,0:T(8,128)(2,1)S(1)}, u32[]{:S(2)}, u32[]{:S(2)}) collective-permute-start(bf16[32,2048]{1,0:T(8,128)(2,1)S(1)} %slice.53), channel_id=1, source_target_pairs={{0,256},{4,260},{8,264},{12,268},{16,272},{20,276},{24,280},{28,28... | collective-permute-start | bytes 393224 | tf_op jit(solution)/shard_map/ppermute | solution.py:14
  21.6 31.1 %copy-start.19 = (s32[512]{0:T(512)S(1)}, s32[512]{0:T(512)}, u32[]{:S(2)}) copy-start(s32[512]{0:T(512)} %constant.144.clone.1) | copy-start | bytes 6148
  21.7 34.3 %collective-permute-start = (bf16[32,2048]{1,0:T(8,128)(2,1)S(1)}, bf16[32,2048]{1,0:T(8,128)(2,1)S(1)}, u32[]{:S(2)}, u32[]{:S(2)}) collective-permute-start(bf16[32,2048]{1,0:T(8,128)(2,1)S(1)} %slice.79), channel_id=1, source_target_pairs={{0,256},{4,260},{8,264},{12,268},{16,272},{20,276},{24,280},{28,28... | collective-permute-start | bytes 393224 | tf_op jit(solution)/shard_map/ppermute | solution.py:14
  29.0 448.3 %reduce-scatter.3.cloned.1.call-start = ((), (), s32[]{:S(2)}) async-start(), calls=%async_computation.4 | async-start | bytes 2621440 | tf_op jit(solution)/shard_map/reduce_scatter | solution.py:159
  31.7 25.0 %copy-start.17 = (pred[32]{0:T(512)(128)(4,1)}, pred[32]{0:T(512)(128)(4,1)S(1)}, u32[]{:S(2)}) copy-start(pred[32]{0:T(512)(128)(4,1)S(1)} %get-tuple-element.36) | copy-start | bytes 100
  31.7 25.0 %copy-start.18 = (pred[32]{0:T(512)(128)(4,1)}, pred[32]{0:T(512)(128)(4,1)S(1)}, u32[]{:S(2)}) copy-start(pred[32]{0:T(512)(128)(4,1)S(1)} %get-tuple-element.37) | copy-start | bytes 100
  45.6 41.4 %collective-permute-start.3 = (bf16[256,2048]{0,1:T(8,128)(2,1)S(1)}, bf16[256,2048]{0,1:T(8,128)(2,1)}, u32[]{:S(2)}, u32[]{:S(2)}) collective-permute-start(bf16[256,2048]{0,1:T(8,128)(2,1)S(1)} %copy.40), channel_id=1, source_target_pairs={{0,256},{4,260},{8,264},{12,268},{16,272},{20,276},{24,280},{28,28... | collective-permute-start | bytes 3145736 | tf_op jit(solution)/shard_map/ppermute | solution.py:14
  56.8 31.5 %copy-start.7 = (bf16[32,2048]{1,0:T(8,128)(2,1)}, bf16[32,2048]{1,0:T(8,128)(2,1)S(1)}, u32[]{:S(2)}) copy-start(bf16[32,2048]{1,0:T(8,128)(2,1)S(1)} %get-tuple-element.22) | copy-start | bytes 393220
  56.8 31.5 %copy-start.10 = (bf16[4,16,8,128]{3,2,1,0:T(8,128)(2,1)}, bf16[4,16,8,128]{3,2,1,0:T(8,128)(2,1)S(1)}, u32[]{:S(2)}) copy-start(bf16[4,16,8,128]{3,2,1,0:T(8,128)(2,1)S(1)} %get-tuple-element.21) | copy-start | bytes 393220
  77.6 10.7 %copy-start.5 = (bf16[256,2048]{0,1:T(8,128)(2,1)}, bf16[256,2048]{0,1:T(8,128)(2,1)S(1)}, u32[]{:S(2)}) copy-start(bf16[256,2048]{0,1:T(8,128)(2,1)S(1)} %copy.38) | copy-start | bytes 3145732
  77.6 55.9 %collective-permute-start.1 = (bf16[256,2048]{0,1:T(8,128)(2,1)S(1)}, bf16[256,2048]{0,1:T(8,128)(2,1)S(1)}, u32[]{:S(2)}, u32[]{:S(2)}) collective-permute-start(bf16[256,2048]{0,1:T(8,128)(2,1)S(1)} %copy.38), channel_id=1, source_target_pairs={{0,256},{4,260},{8,264},{12,268},{16,272},{20,276},{24,280},{28,28... | collective-permute-start | bytes 3145736 | tf_op jit(solution)/shard_map/ppermute | solution.py:14
  85.6 2.8 copy-start.13
  88.3 1.7 copy-start.2
  88.4 45.2 %copy-start.6 = (bf16[256,2048]{0,1:T(8,128)(2,1)S(1)}, bf16[256,2048]{0,1:T(8,128)(2,1)}, u32[]{:S(2)}) copy-start(bf16[256,2048]{0,1:T(8,128)(2,1)} %copy-done.5) | copy-start | bytes 3145732
  88.8 1.6 copy-start.4
  152.1 43.4 %collective-permute-start.7 = (f32[256,2048]{1,0:T(8,128)}, f32[256,2048]{1,0:T(8,128)}, u32[]{:S(2)}, u32[]{:S(2)}) collective-permute-start(f32[256,2048]{1,0:T(8,128)} %copy.50), channel_id=1, source_target_pairs={{0,256},{4,260},{8,264},{12,268},{16,272},{20,276},{24,280},{28,28... | collective-permute-start | bytes 6291464 | tf_op jit(solution)/shard_map/ppermute | solution.py:14
  198.9 278.4 %reduce-scatter.5.cloned.1.call-start = ((), (), s32[]{:S(2)}) async-start(), calls=%async_computation.5 | async-start | bytes 2621440 | tf_op jit(solution)/shard_map/reduce_scatter | solution.py:160
  209.6 74.2 %collective-permute-start.8 = (f32[256,2048]{1,0:T(8,128)}, f32[256,2048]{1,0:T(8,128)}, u32[]{:S(2)}, u32[]{:S(2)}) collective-permute-start(f32[256,2048]{1,0:T(8,128)} %copy.53), channel_id=1, source_target_pairs={{0,256},{4,260},{8,264},{12,268},{16,272},{20,276},{24,280},{28,28... | collective-permute-start | bytes 6291464 | tf_op jit(solution)/shard_map/ppermute | solution.py:14
  287.1 2.4 copy-start.3
  289.5 7.0 %copy-start.8 = (bf16[32,2048]{1,0:T(8,128)(2,1)S(1)}, bf16[32,2048]{1,0:T(8,128)(2,1)}, u32[]{:S(2)}) copy-start(bf16[32,2048]{1,0:T(8,128)(2,1)} %copy-done.7) | copy-start | bytes 393220
  294.8 3.3 copy-start.21
  294.8 12.7 %copy-start.15 = (f32[32]{0:T(128)S(1)}, f32[32]{0:T(128)}, u32[]{:S(2)}) copy-start(f32[32]{0:T(128)} %get-tuple-element.35) | copy-start | bytes 388
  294.8 12.7 %copy-start.16 = (f32[32]{0:T(128)S(1)}, f32[32]{0:T(128)}, u32[]{:S(2)}) copy-start(f32[32]{0:T(128)} %get-tuple-element.17) | copy-start | bytes 388
  296.5 180.8 %copy-start.20 = (pred[64]{0:T(512)(128)(4,1)S(1)}, pred[64]{0:T(512)(128)(4,1)}, u32[]{:S(2)}) copy-start(pred[64]{0:T(512)(128)(4,1)} %iota_compare_fusion.2) | copy-start | bytes 196
  298.2 179.1 %collective-permute-start.6 = (bf16[32,2048]{1,0:T(8,128)(2,1)S(1)}, bf16[32,2048]{1,0:T(8,128)(2,1)S(1)}, u32[]{:S(2)}, u32[]{:S(2)}) collective-permute-start(bf16[32,2048]{1,0:T(8,128)(2,1)S(1)} %get-tuple-element.28), channel_id=1, source_target_pairs={{0,256},{4,260},{8,264},{12,268},{16,272},{20,276},{24,280},{28,28... | collective-permute-start | bytes 393224 | tf_op jit(solution)/shard_map/ppermute | solution.py:14
  300.1 175.4 %collective-permute-start.4 = (bf16[32,2048]{1,0:T(8,128)(2,1)S(1)}, bf16[32,2048]{1,0:T(8,128)(2,1)S(1)}, u32[]{:S(2)}, u32[]{:S(2)}) collective-permute-start(bf16[32,2048]{1,0:T(8,128)(2,1)S(1)} %get-tuple-element.29), channel_id=1, source_target_pairs={{0,256},{4,260},{8,264},{12,268},{16,272},{20,276},{24,280},{28,28... | collective-permute-start | bytes 393224 | tf_op jit(solution)/shard_map/ppermute | solution.py:14
  477.3 2.6 copy-start.1
Sparse Core Ops, SparseCore 0:
  10.2 33.8 all-gather.4
  46.2 29.9 all-gather.2
  199.0 118.6 reduce-scatter.2
  320.7 68.3 reduce-scatter.4
where the time goes:
time: 487 us; the launch traced here: 486 us
  waiting for transfers between devices  175 us (36%)
  blocking collectives  168 us (34%)
  starting transfers between devices  55.9 us (11%)
  local copies, waits for them, and re-layouts  28.8 us (6%)
  matrix products  22.2 us (5%)
  other arithmetic  20.9 us (4%)
  between operations  15.6 us (3%)
    psum x1, blocking collectives, shards(): router_total = lax.psum(d_router, ('dp', 'seq'))  168 us
    ppermute x9, waiting for transfers between devices, swapped(): return lax.ppermute(value, axis, pairs)  143 us
    ppermute x9, starting transfers between devices, swapped(): return lax.ppermute(value, axis, pairs)  55.7 us
    all_gather x1, waiting for transfers between devices, shards(): lax.all_gather(value_proj, 'seq', axis=0, tiled=True)  19.3 us
    all_gather x1, waiting for transfers between devices, shards(): lax.all_gather(key_proj, 'seq', axis=0, tiled=True)  12.3 us
  transfers between devices with their start and end apart: 13, of which 6 were waited for; matrix products, arithmetic and copies ran while one was open for 9% of the time, Pallas kernels for 0%

commit v1 on v0

v1 whole, which is shorter than its diff:
```python
import functools
import math

import jax
import jax.numpy as jnp
from jax import lax
from jax.experimental import pallas as pl
from jax.experimental.pallas import tpu as pltpu
from jax.sharding import Mesh
from jax.sharding import PartitionSpec as P

HEADS = 16
LANES = 128
CORES = 2
MIB = 1024 * 1024
VMEM = pl.BlockSpec(memory_space=pltpu.VMEM)
SMEM = pl.BlockSpec(memory_space=pltpu.SMEM)


def flipped(row):
    n = row.shape[1]
    down = lax.broadcasted_iota(jnp.int32, (n, n), 0)
    along = lax.broadcasted_iota(jnp.int32, (n, n), 1)
    return jnp.sum(jnp.where(down == along, row, 0.0), axis=1, keepdims=True)


def prep_kernel(place, counts, rows, residual, queries, keys, values, grads, router, sent, picked, gates):
    slots, width = queries.shape
    groups = sent.shape[0]
    part = width // groups
    tokens = residual.shape[0]
    own = rows[0, pl.ds(place[1], 1), :].astype(jnp.float32)
    slot = lax.broadcasted_iota(jnp.int32, (slots, 1), 0)
    live = slot < counts[place[0], place[1]]
    token = lax.broadcasted_iota(jnp.int32, (slots, tokens), 1).astype(jnp.float32)
    pick = (flipped(own) == token).astype(jnp.bfloat16)
    x = jnp.dot(pick, residual[...], preferred_element_type=jnp.float32)
    picked[...] = x.astype(jnp.bfloat16)
    gate = jax.nn.sigmoid(jnp.sum(x * router[...], axis=1, keepdims=True))
    gates[...] = jnp.broadcast_to(gate, gates.shape)
    d_att = (jnp.where(live, gate, 0.0) * grads[...].astype(jnp.float32)).astype(jnp.bfloat16)
    for group in range(groups):
        columns = slice(group * part, (group + 1) * part)
        sent[group, 0] = queries[:, columns]
        sent[group, 1] = keys[:, columns]
        sent[group, 2] = values[:, columns]
        sent[group, 3] = d_att[:, columns]


def attend_kernel(place, counts, rows, got, sent, *, tok_dev):
    blocks, _, slots, part = got.shape
    n = blocks * slots
    spread = (
        lax.broadcasted_iota(jnp.int32, (slots, n), 1) % slots
        == lax.broadcasted_iota(jnp.int32, (slots, n), 0)
    ).astype(jnp.float32)
    tiled = jnp.dot(rows[0].astype(jnp.float32), spread, preferred_element_type=jnp.float32)
    along = lax.broadcasted_iota(jnp.int32, (1, n), 1)
    k_block, k_slot = along // slots, along % slots
    k_pos = jnp.zeros((1, n), jnp.float32)
    k_count = jnp.zeros((1, n), jnp.int32)
    for block in range(blocks):
        here = k_block == block
        k_pos = jnp.where(here, tiled[block : block + 1] + float(block * tok_dev), k_pos)
        k_count = jnp.where(here, counts[place[0], block], k_count)
    allowed = (k_pos <= flipped(k_pos)) & (k_slot < k_count)
    inv_scale = 1.0 / math.sqrt(LANES)
    mm = functools.partial(lax.dot_general, preferred_element_type=jnp.float32)
    for head in range(part // LANES):
        columns = slice(head * LANES, (head + 1) * LANES)
        q, k, v, da = (got[:, i, :, columns].reshape(n, LANES) for i in range(4))
        scores = mm(q, k, (((1,), (1,)), ((), ()))) * inv_scale
        scores = jnp.where(allowed, scores, -1e30)
        e = jnp.exp(scores - jnp.max(scores, axis=1, keepdims=True))
        probs = e * (1.0 / jnp.sum(e, axis=1, keepdims=True))
        low = probs.astype(jnp.bfloat16)
        att = mm(low, v, (((1,), (0,)), ((), ())))
        d_probs = mm(da, v, (((1,), (1,)), ((), ())))
        d_scores = probs * (d_probs - jnp.sum(probs * d_probs, axis=1, keepdims=True)) * inv_scale
        d_scores = d_scores.astype(jnp.bfloat16)
        dq = mm(d_scores, k, (((1,), (0,)), ((), ())))
        dk = mm(d_scores, q, (((0,), (0,)), ((), ())))
        dv = mm(low, da, (((0,), (0,)), ((), ())))
        for i, value in enumerate((att, dq, dk, dv)):
            sent[:, i, :, columns] = value.astype(jnp.bfloat16).reshape(blocks, slots, LANES)


def finish_kernel(
    place, counts, rows, got, residual, grads, picked, gates, block_out, d_queries, d_keys, d_values, d_router
):
    groups, _, slots, part = got.shape
    tokens, width = residual.shape
    count = counts[place[0], place[1]]
    live = lax.broadcasted_iota(jnp.int32, (slots, 1), 0) < count
    gate = gates[:, :1]
    d_gate = jnp.zeros((slots, 1), jnp.float32)
    for group in range(groups):
        columns = slice(group * part, (group + 1) * part)
        att = got[group, 0].astype(jnp.float32)
        d_gate += jnp.sum(grads[:, columns].astype(jnp.float32) * att, axis=1, keepdims=True)
    d_logit = jnp.where(live, d_gate * gate * (1.0 - gate), 0.0)
    x = picked[...].astype(jnp.float32)
    term = jnp.sum(d_logit * x, axis=0, keepdims=True)
    for k in range(width // LANES):
        piece = term[:, k * LANES : (k + 1) * LANES]
        d_router[:, k : k + 1, :] = jnp.broadcast_to(piece[None], (d_router.shape[0], 1, LANES))
    own = rows[0, pl.ds(place[1], 1), :].astype(jnp.float32)
    along = lax.broadcasted_iota(jnp.int32, (1, slots), 1)
    own = jnp.where(along < count, own, -1.0)
    token = lax.broadcasted_iota(jnp.int32, (tokens, slots), 0).astype(jnp.float32)
    put = (token == own).astype(jnp.float32)
    hit = jnp.sum(put, axis=1, keepdims=True) > 0.0
    put = put.astype(jnp.bfloat16)
    for group in range(groups):
        columns = slice(group * part, (group + 1) * part)
        att = got[group, 0].astype(jnp.float32)
        mixed = (x[:, columns] + gate * att).astype(jnp.bfloat16)
        moved = jnp.dot(put, mixed, preferred_element_type=jnp.float32).astype(jnp.bfloat16)
        block_out[:, columns] = jnp.where(hit, moved, residual[:, columns])
        for i, out in enumerate((d_queries, d_keys, d_values)):
            out[:, columns] = jnp.where(live, got[group, 1 + i], jnp.zeros((), jnp.bfloat16))


def call(kernel, out_shape, place, counts, rows, *operands, flops):
    slots = rows.shape[2]
    blocks = rows.shape[1]

    def whole(array):
        return pl.BlockSpec(array.shape, lambda i, *_: (0,) * len(array.shape))

    outs = jax.tree.map(whole, out_shape)
    moved = sum(o.size * o.dtype.itemsize for o in (*operands, *jax.tree.leaves(out_shape)))
    return pl.pallas_call(
        kernel,
        out_shape=out_shape,
        grid_spec=pltpu.PrefetchScalarGridSpec(
            num_scalar_prefetch=2,
            grid=(1,),
            in_specs=[pl.BlockSpec((1, blocks, slots), lambda i, place, counts: (place[0], 0, 0))]
            + [whole(o) for o in operands],
            out_specs=outs,
        ),
        compiler_params=pltpu.CompilerParams(vmem_limit_bytes=40 * MIB),
        cost_estimate=pl.CostEstimate(flops=flops, bytes_accessed=moved, transcendentals=0),
    )(place, counts, rows, *operands)


def shards(residual, queries, keys, values, grads, router, counts, rows, *, sizes):
    n_y, n_z, n_c, groups = sizes
    tok_dev, width = residual.shape
    slots = queries.shape[0]
    part = width // groups
    bf16, f32 = jnp.bfloat16, jnp.float32
    dp_index = (lax.axis_index("y") * n_z + lax.axis_index("z")) * n_c + lax.axis_index("c")
    place = jnp.stack([dp_index, lax.axis_index("x")]).astype(jnp.int32)
    shape = jax.ShapeDtypeStruct
    packed = shape((groups, 4, slots, part), bf16)
    sent, picked, gates = call(
        prep_kernel,
        (packed, shape((slots, width), bf16), shape((slots, LANES), f32)),
        place, counts, rows, residual, queries, keys, values, grads, router.reshape(1, width),
        flops=2 * slots * tok_dev * width,
    )
    got = lax.all_to_all(sent, "x", 0, 0)
    back = call(
        functools.partial(attend_kernel, tok_dev=tok_dev),
        packed, place, counts, rows, got,
        flops=12 * (groups * slots) ** 2 * part,
    )
    back = lax.all_to_all(back, "x", 0, 0)
    wide = shape((slots, width), bf16)
    block_out, d_queries, d_keys, d_values, term = call(
        finish_kernel,
        (shape((tok_dev, width), bf16), wide, wide, wide, shape((n_c * groups, width // LANES, LANES), f32)),
        place, counts, rows, back, residual, grads, picked, gates,
        flops=2 * slots * tok_dev * width,
    )
    total = jnp.sum(lax.all_to_all(term, ("c", "x"), 0, 0), axis=0)
    for axis, size in (("y", n_y), ("z", n_z)):
        copies = jnp.broadcast_to(total[None], (size, *total.shape))
        total = jnp.sum(lax.all_to_all(copies, axis, 0, 0), axis=0)
    return block_out, d_queries, d_keys, d_values, total.reshape(width)


def split_dp(size):
    chips = size // CORES
    z = 2 ** (int(math.log2(chips)) // 2)
    return chips // z, z, CORES


def solution(mesh):
    sizes = (*split_dp(mesh.shape["dp"]), mesh.shape["seq"])
    fine = Mesh(mesh.devices.reshape(sizes), ("y", "z", "c", "x"))
    split = P(("y", "z", "c", "x"), None)
    return jax.shard_map(
        functools.partial(shards, sizes=sizes),
        mesh=fine,
        in_specs=(split,) * 5 + (P(),) * 3,
        out_specs=(split,) * 4 + (P(),),
        check_vma=False,
    )
```

time: 487 us -> 94.8 us (0.19)
  waiting for transfers between devices: 175 us -> 0 us
  blocking collectives: 168 us -> 75.7 us
  starting transfers between devices: 55.9 us -> 0 us
  local copies, waits for them, and re-layouts: 28.8 us -> 6.57 us
  matrix products: 22.2 us -> 0 us
  other arithmetic: 20.9 us -> 0.71 us
  between operations: 15.6 us -> 0.73 us
  Pallas kernels: 0 us -> 9.63 us
    psum x1 -> x0, blocking collectives: 168 us -> none  [shards(): router_total = lax.psum(d_router, ('dp', 'seq'))]
    ppermute x9 -> x0, waiting for transfers between devices: 143 us -> none  [swapped(): return lax.ppermute(value, axis, pairs)]
    all_to_all x0 -> x5, blocking collectives: none -> 75.7 us  [the longest x2 34.2 us: shards(): total = jnp.sum(lax.all_to_all(copies, axis, 0, 0), axis=0)]
    ppermute x9 -> x0, starting transfers between devices: 55.7 us -> none  [swapped(): return lax.ppermute(value, axis, pairs)]
    all_gather x2 -> x0, waiting for transfers between devices: 31.6 us -> none  [the longest x1 19.3 us: shards(): lax.all_gather(value_proj, 'seq', axis=0, tiled=True)]
    dot_general x8 -> x0, matrix products: 22.2 us -> none  [the longest x1 6.83 us: attend_rows(): jnp.einsum('hqk,qhd->khd', d_scores, qh, preferred_element_type=jnp.float32)]
    slice x10 -> x0, local copies, waits for them, and re-layouts: 15.7 us -> none  [the longest x2 5.84 us: shards(): d_value[n_keys:]]
    pallas_call x0 -> x3, Pallas kernels: none -> 9.63 us  [call(): pl.pallas_call(kernel, out_shape=out_shape, grid_spec=pltpu.PrefetchScala...]
  transfers between devices with their start and end apart: 13 -> 0, of which waited for: 6 -> 0; matrix products, arithmetic and copies ran while one was open for 9% -> 0% of each run, Pallas kernels for 0% -> 0%
where the time goes in v1:
time: 94.8 us; the launch traced here: 93.3 us
  blocking collectives  75.7 us (80%)
  Pallas kernels  9.63 us (10%)
  local copies, waits for them, and re-layouts  6.57 us (7%)
    all_to_all x2, blocking collectives, shards(): total = jnp.sum(lax.all_to_all(copies, axis, 0, 0), axis=0)  34.2 us
    all_to_all x1, blocking collectives, shards(): got = lax.all_to_all(sent, 'x', 0, 0)  15.1 us
    all_to_all x1, blocking collectives, shards(): total = jnp.sum(lax.all_to_all(term, ('c', 'x'), 0, 0), axis=0)  14.1 us
    all_to_all x1, blocking collectives, shards(): back = lax.all_to_all(back, 'x', 0, 0)  12.3 us
    pallas_call x3, Pallas kernels, call(): pl.pallas_call(kernel, out_shape=out_shape, grid_spec=pltpu.PrefetchScala...  9.63 us
    unnamed x16, local copies, waits for them, and re-layouts  6.56 us

profile of v1, /device:TPU:1, one launch (start us, length us, event | category | flops | bytes accessed | tf_op | source)
XLA Modules:
  0.0 93.3 jit_solution(207459242965635446)
XLA Ops:
  0.6 0.0 copy-start.2
  0.6 0.8 copy.23.counts
  1.5 1.0 %copy.24.rows = s32[128,4,64]{2,1,0:T(4,128)S(1)} copy(s32[128,4,64]{0,2,1:T(8,128)} %param.15) | data formatting | bytes 262144 | tf_op args[7]
  2.5 0.0 copy-start.6
  2.6 0.1 pad_add_fusion.place
  2.6 0.0 copy-done.2
  2.6 0.6 copy-done.6
  3.2 0.0 copy-start
  3.2 1.2 %copy-done = bf16[256,2048]{1,0:T(8,128)(2,1)S(1)} copy-done((bf16[256,2048]{1,0:T(8,128)(2,1)S(1)}, bf16[256,2048]{1,0:T(8,128)(2,1)}, u32[]{:S(2)}) %copy-start) | copy-done | bytes 1048600
  4.5 0.0 copy-start.3
  4.5 0.9 %copy-done.3 = bf16[64,2048]{1,0:T(8,128)(2,1)S(1)} copy-done((bf16[64,2048]{1,0:T(8,128)(2,1)S(1)}, bf16[64,2048]{1,0:T(8,128)(2,1)}, u32[]{:S(2)}) %copy-start.3) | copy-done | bytes 262168
  5.4 0.0 copy-start.4
  5.4 0.9 %copy-done.4 = bf16[64,2048]{1,0:T(8,128)(2,1)S(1)} copy-done((bf16[64,2048]{1,0:T(8,128)(2,1)S(1)}, bf16[64,2048]{1,0:T(8,128)(2,1)}, u32[]{:S(2)}) %copy-start.4) | copy-done | bytes 262168
  6.4 0.0 copy-start.5
  6.4 0.9 %copy-done.5 = bf16[64,2048]{1,0:T(8,128)(2,1)S(1)} copy-done((bf16[64,2048]{1,0:T(8,128)(2,1)S(1)}, bf16[64,2048]{1,0:T(8,128)(2,1)}, u32[]{:S(2)}) %copy-start.5) | copy-done | bytes 262168
  7.3 2.1 %shard_map.119 = (bf16[4,4,64,512]{3,2,1,0:T(8,128)(2,1)S(1)}, bf16[64,2048]{1,0:T(8,128)(2,1)S(1)}, f32[64,128]{1,0:T(8,128)S(1)}) custom-call(s32[2]{0:T(128)S(1)} %pad_add_fusion.place, s32[128,4]{1,0:T(8,128)S(1)} %copy.23.counts, s32[128,4,64]{2,1,0:T(4,128)S(1)} %copy.24.rows, bf16[256,2048]{1,0:T(8,128)(2,1)S(1)} %copy-done, ...), custom_call_target="tpu_custom_call" | custom-call | flops 67108864 | bytes 3448832 | tf_op jit(solution)/shard_map/pallas_call | solution.py:133
  9.4 15.1 %all_to_all.25.got = bf16[4,4,64,512]{3,2,1,0:T(8,128)(2,1)S(1)} all-to-all(bf16[4,4,64,512]{3,2,1,0:T(8,128)(2,1)S(1)} %get-tuple-element.13), channel_id=1, replica_groups=mesh['y'=8,'z'=8,'c'=2,'x'=4] {'x'}, dimensions={0} | all-to-all | bytes 2097152 | tf_op jit(solution)/shard_map/all_to_all | solution.py:164
  24.5 4.3 %shard_map.120 = bf16[4,4,64,512]{3,2,1,0:T(8,128)(2,1)S(1)} custom-call(s32[2]{0:T(128)S(1)} %pad_add_fusion.place, s32[128,4]{1,0:T(8,128)S(1)} %copy.23.counts, s32[128,4,64]{2,1,0:T(4,128)S(1)} %copy.24.rows, bf16[4,4,64,512]{3,2,1,0:T(8,128)(2,1)S(1)} %all_to_all.25.got), custom_call_target="tpu_custom_call" | custom-call | flops 402653184 | bytes 2097152 | tf_op jit(solution)/shard_map/pallas_call | solution.py:133
  28.9 0.0 copy-start.1
  28.9 12.3 %all_to_all.26.got = bf16[4,4,64,512]{3,2,1,0:T(8,128)(2,1)S(1)} all-to-all(bf16[4,4,64,512]{3,2,1,0:T(8,128)(2,1)S(1)} %shard_map.120), channel_id=1, replica_groups=mesh['y'=8,'z'=8,'c'=2,'x'=4] {'x'}, dimensions={0} | all-to-all | bytes 2097152 | tf_op jit(solution)/shard_map/all_to_all | solution.py:170
  41.2 0.0 copy-done.1
  41.2 3.2 %shard_map.121 = (bf16[256,2048]{1,0:T(8,128)(2,1)}, bf16[64,2048]{1,0:T(8,128)(2,1)}, bf16[64,2048]{1,0:T(8,128)(2,1)}, bf16[64,2048]{1,0:T(8,128)(2,1)}, f32[8,16,128]{2,1,0:T(8,128)S(1)}) custom-call(s32[2]{0:T(128)S(1)} %pad_add_fusion.place, s32[128,4]{1,0:T(8,128)S(1)} %copy.23.counts, s32[128,4,64]{2,1,0:T(4,128)S(1)} %copy.24.rows, ...), custom_call_target="tpu_custom_call" | custom-call | flops 67108864 | bytes 4554752 | tf_op jit(solution)/shard_map/pallas_call | solution.py:133
  44.4 14.1 %all_to_all.27 = f32[8,16,128]{2,1,0:T(8,128)S(1)} all-to-all(f32[8,16,128]{2,1,0:T(8,128)S(1)} %get-tuple-element.20), channel_id=1, replica_groups=mesh['y'=8,'z'=8,'c'=2,'x'=4] {'c','x'}, dimensions={0} | all-to-all | bytes 131072 | tf_op jit(solution)/shard_map/all_to_all | solution.py:178
  58.5 17.1 %all_to_all.28 = f32[8,16,128]{2,1,0:T(8,128)S(1)} all-to-all(f32[8,16,128]{2,1,0:T(8,128)S(1)} %broadcast_in_dim.4), channel_id=1, replica_groups=mesh['y'=8,'z'=8,'c'=2,'x'=4] {'y'}, dimensions={0} | all-to-all | bytes 131072 | tf_op jit(solution)/shard_map/all_to_all | solution.py:181
  75.6 17.1 %all_to_all.29 = f32[8,16,128]{2,1,0:T(8,128)S(1)} all-to-all(f32[8,16,128]{2,1,0:T(8,128)S(1)} %broadcast_in_dim.5), channel_id=1, replica_groups=mesh['y'=8,'z'=8,'c'=2,'x'=4] {'z'}, dimensions={0} | all-to-all | bytes 131072 | tf_op jit(solution)/shard_map/all_to_all | solution.py:181
  92.7 0.6 reduce_sum.29
  (4 shorter events, 0.0 us)
Async XLA Ops:
  0.6 2.0 %copy-start.2 = (bf16[64,2048]{1,0:T(8,128)(2,1)S(1)}, bf16[64,2048]{1,0:T(8,128)(2,1)}, u32[]{:S(2)}) copy-start(bf16[64,2048]{1,0:T(8,128)(2,1)} %grads.3) | copy-start | bytes 786436
  2.5 0.7 copy-start.6
  3.2 1.2 %copy-start = (bf16[256,2048]{1,0:T(8,128)(2,1)S(1)}, bf16[256,2048]{1,0:T(8,128)(2,1)}, u32[]{:S(2)}) copy-start(bf16[256,2048]{1,0:T(8,128)(2,1)} %residual.3) | copy-start | bytes 3145732
  4.5 0.9 %copy-start.3 = (bf16[64,2048]{1,0:T(8,128)(2,1)S(1)}, bf16[64,2048]{1,0:T(8,128)(2,1)}, u32[]{:S(2)}) copy-start(bf16[64,2048]{1,0:T(8,128)(2,1)} %queries.1) | copy-start | bytes 786436
  5.4 0.9 %copy-start.4 = (bf16[64,2048]{1,0:T(8,128)(2,1)S(1)}, bf16[64,2048]{1,0:T(8,128)(2,1)}, u32[]{:S(2)}) copy-start(bf16[64,2048]{1,0:T(8,128)(2,1)} %keys.1) | copy-start | bytes 786436
  6.4 0.9 %copy-start.5 = (bf16[64,2048]{1,0:T(8,128)(2,1)S(1)}, bf16[64,2048]{1,0:T(8,128)(2,1)}, u32[]{:S(2)}) copy-start(bf16[64,2048]{1,0:T(8,128)(2,1)} %values.1) | copy-start | bytes 786436
  28.9 12.3 %copy-start.1 = (bf16[256,2048]{1,0:T(8,128)(2,1)S(1)}, bf16[256,2048]{1,0:T(8,128)(2,1)}, u32[]{:S(2)}) copy-start(bf16[256,2048]{1,0:T(8,128)(2,1)} %residual.3) | copy-start | bytes 3145732

commit v2 on v1

v2 whole, which is shorter than its diff:
```python
import functools
import math

import jax
import jax.numpy as jnp
from jax import lax
from jax.experimental import pallas as pl
from jax.experimental.pallas import tpu as pltpu
from jax.sharding import Mesh
from jax.sharding import PartitionSpec as P

HEADS = 16
LANES = 128
CORES = 2
MIB = 1024 * 1024
ORDER = (("y", lambda s: s[0]), (("c", "x"), lambda s: s[2] * s[3]), ("z", lambda s: s[1]))
VMEM = pl.BlockSpec(memory_space=pltpu.VMEM)
ANY = pl.BlockSpec(memory_space=pl.ANY)
HBM = pl.BlockSpec(memory_space=pltpu.HBM)


def sequence_index(sizes):
    _, n_z, n_c, _ = sizes
    return (lax.axis_index("y") * n_z + lax.axis_index("z")) * n_c + lax.axis_index("c")


def column(table, index):
    lane = lax.broadcasted_iota(jnp.int32, table.shape, 1)
    return jnp.sum(jnp.where(lane == index, table, 0), axis=1, keepdims=True).astype(jnp.float32)


def prep_kernel(
    residual, queries, keys, values, grads, router, counts, rows, sent, picked, marks,
    residual_v, grads_v, straight_v, router_v, counts_v, rows_v, d_att_v, sems, *, sizes,
):
    slots, width = queries.shape
    groups, _, _, part = sent.shape
    tokens = residual.shape[0]
    dp_index, block_index = sequence_index(sizes), lax.axis_index("x")

    def fetch(source, target, i):
        copy = pltpu.make_async_copy(source, target, sems.at[i])
        copy.start()
        return copy

    small = [fetch(rows.at[block_index], rows_v, 0), fetch(counts, counts_v, 1), fetch(router, router_v, 2)]
    wide = [fetch(residual, residual_v, 3), fetch(grads, grads_v, 4)]
    pieces = [pl.ds(group * part, part) for group in range(groups)]
    straight = [fetch(array, straight_v.at[i], 5 + i) for i, array in enumerate((queries, keys, values))]
    for copy in small:
        copy.wait()
    count = column(counts_v[...], dp_index)
    own_block = lax.broadcasted_iota(jnp.int32, count.shape, 0) == block_index
    count = jnp.sum(jnp.where(own_block, count, 0.0), axis=0, keepdims=True)
    live = lax.broadcasted_iota(jnp.int32, (slots, 1), 0).astype(jnp.float32) < count
    token = lax.broadcasted_iota(jnp.int32, (slots, tokens), 1).astype(jnp.float32)
    pick = (column(rows_v[...], dp_index) == token).astype(jnp.bfloat16)
    wide[0].wait()
    x = jnp.dot(pick, residual_v[...], preferred_element_type=jnp.float32)
    picked[...] = x.astype(jnp.bfloat16)
    gate = jax.nn.sigmoid(jnp.sum(x * router_v[...], axis=1, keepdims=True))
    lane = lax.broadcasted_iota(jnp.int32, marks.shape, 1)
    marks[...] = jnp.where(lane == 0, gate, live.astype(jnp.float32))
    copies = []
    for i, copy in enumerate(straight):
        copy.wait()
        for group in range(groups):
            copies.append(fetch(straight_v.at[i, :, pieces[group]], sent.at[group, i], 8 + 4 * group + i))
    wide[1].wait()
    gate = jnp.where(live, gate, 0.0)
    for group in range(groups):
        columns = slice(group * part, (group + 1) * part)
        d_att_v[group] = (gate * grads_v[:, columns].astype(jnp.float32)).astype(jnp.bfloat16)
        copies.append(fetch(d_att_v.at[group], sent.at[group, 3], 11 + 4 * group))
    for copy in copies:
        copy.wait()


def mask_kernel(counts, rows, mask, places, *, sizes, tok_dev):
    blocks, slots, _ = rows.shape
    n = blocks * slots
    dp_index, block_index = sequence_index(sizes), lax.axis_index("x")
    row = column(rows[...].reshape(n, rows.shape[2]), dp_index)
    count = column(counts[...], dp_index)
    slot = lax.broadcasted_iota(jnp.int32, (n, 1), 0)
    block = slot // slots
    counted = jnp.zeros((n, 1), jnp.float32)
    for b in range(blocks):
        counted = jnp.where(block == b, count[b : b + 1], counted)
    live = (slot % slots).astype(jnp.float32) < counted
    position = row + (block * tok_dev).astype(jnp.float32)
    down = lax.broadcasted_iota(jnp.int32, (n, n), 0)
    along = lax.broadcasted_iota(jnp.int32, (n, n), 1)
    seen = jnp.where(live, position, float(blocks * tok_dev))
    seen = jnp.sum(jnp.where(down == along, seen, 0.0), axis=0, keepdims=True)
    mask[...] = (seen <= position).astype(jnp.float32)
    own = jnp.where(live & (block == block_index), row + 1.0, 0.0)
    down = lax.broadcasted_iota(jnp.int32, (n, LANES), 0) % slots
    along = lax.broadcasted_iota(jnp.int32, (n, LANES), 1)
    own = jnp.sum(jnp.where(down == along, own, 0.0), axis=0, keepdims=True) - 1.0
    places[...] = jnp.broadcast_to(own, places.shape)


def forward_kernel(got, mask, attended, probs, dots):
    blocks, _, slots, part = got.shape
    n = blocks * slots
    allowed = mask[...] > 0.0
    inv_scale = 1.0 / math.sqrt(LANES)
    mm = functools.partial(lax.dot_general, preferred_element_type=jnp.float32)
    dot = jnp.zeros((n, LANES), jnp.float32)
    for head in range(part // LANES):
        columns = slice(head * LANES, (head + 1) * LANES)
        q, k, v, da = (got[:, i, :, columns].reshape(n, LANES) for i in range(4))
        scores = mm(q, k, (((1,), (1,)), ((), ()))) * inv_scale
        scores = jnp.where(allowed, scores, -1e30)
        e = jnp.exp(scores - jnp.max(scores, axis=1, keepdims=True))
        weights = e * (1.0 / jnp.sum(e, axis=1, keepdims=True))
        probs[head] = weights
        att = mm(weights.astype(jnp.bfloat16), v, (((1,), (0,)), ((), ())))
        attended[:, columns] = att.astype(jnp.bfloat16)
        dot += att * da.astype(jnp.float32)
    ones = jnp.ones((8, LANES), jnp.float32)
    dot = mm(ones, dot, (((1,), (1,)), ((), ())), precision=lax.Precision.HIGHEST)
    dots[...] = jnp.broadcast_to(dot[None], dots.shape)


def backward_kernel(got, attended, probs, *refs):
    blocks, _, slots, part = got.shape
    *outs, held, sems = refs
    n = blocks * slots
    inv_scale = 1.0 / math.sqrt(LANES)
    mm = functools.partial(lax.dot_general, preferred_element_type=jnp.float32)
    for head in range(part // LANES):
        columns = slice(head * LANES, (head + 1) * LANES)
        q, k, v, da = (got[:, i, :, columns].reshape(n, LANES) for i in range(4))
        weights = probs[head]
        d_probs = mm(da, v, (((1,), (1,)), ((), ())))
        d_scores = weights * (d_probs - jnp.sum(weights * d_probs, axis=1, keepdims=True)) * inv_scale
        d_scores = d_scores.astype(jnp.bfloat16)
        dq = mm(d_scores, k, (((1,), (0,)), ((), ())))
        dk = mm(d_scores, q, (((0,), (0,)), ((), ())))
        dv = mm(weights.astype(jnp.bfloat16), da, (((0,), (0,)), ((), ())))
        for i, value in enumerate((dq, dk, dv)):
            held[:, i, :, columns] = value.astype(jnp.bfloat16).reshape(blocks, slots, LANES)
    copies = []
    for distance, out in enumerate(outs):
        block = lax.rem(lax.axis_index("x") + distance, blocks)
        first = pl.multiple_of(block * slots, slots)
        copies.append(pltpu.make_async_copy(attended.at[pl.ds(first, slots), :], out.at[0], sems.at[2 * distance]))
        copies.append(pltpu.make_async_copy(held.at[block], out.at[pl.ds(1, 3)], sems.at[2 * distance + 1]))
    for copy in copies:
        copy.start()
    for copy in copies:
        copy.wait()


def router_kernel(dots, picked, marks, after, d_router):
    slots, width = picked.shape
    n = dots.shape[2]
    dot = jnp.sum(dots[...], axis=0)[0:1]
    first = lax.axis_index("x") * slots
    mine = lax.broadcasted_iota(jnp.int32, (slots, n), 0) + first
    dot = jnp.where(mine == lax.broadcasted_iota(jnp.int32, (slots, n), 1), dot, 0.0)
    d_logit = jnp.sum(dot, axis=1, keepdims=True) * (1.0 - marks[:, 0:1])
    term = jnp.sum(d_logit * picked[...].astype(jnp.float32), axis=0, keepdims=True)
    d_router[...] = jnp.broadcast_to(term[None], d_router.shape)


def finish_kernel(*refs):
    groups = lax.axis_size("x")
    got = refs[:groups]
    residual, picked, marks, places, block_out, d_queries, d_keys, d_values, block_v, lists_v, sems = refs[groups:]
    _, slots, part = got[0].shape
    tokens, width = residual.shape
    gate, live = marks[:, 0:1], marks[:, 1:2] > 0.0
    own = places[0:1, :slots]
    token = lax.broadcasted_iota(jnp.int32, (tokens, slots), 0).astype(jnp.float32)
    put = (token == own).astype(jnp.float32)
    hit = jnp.sum(put, axis=1, keepdims=True) > 0.0
    put = put.astype(jnp.bfloat16)
    copies = []

    def store(source, target):
        copy = pltpu.make_async_copy(source, target, sems.at[len(copies)])
        copy.start()
        copies.append(copy)

    for distance in range(groups):
        group = lax.rem(lax.axis_index("x") + (groups - distance), groups)
        columns = pl.ds(pl.multiple_of(group * part, part), part)
        for i, out in enumerate((d_queries, d_keys, d_values)):
            lists_v[i, distance] = jnp.where(live, got[distance][1 + i], jnp.zeros((), jnp.bfloat16))
            store(lists_v.at[i, distance], out.at[:, columns])
        att = got[distance][0].astype(jnp.float32)
        mixed = (picked[:, columns].astype(jnp.float32) + gate * att).astype(jnp.bfloat16)
        moved = jnp.dot(put, mixed, preferred_element_type=jnp.float32).astype(jnp.bfloat16)
        block_v[distance] = jnp.where(hit, moved, residual[:, columns])
        store(block_v.at[distance], block_out.at[:, columns])
    for copy in copies:
        copy.wait()


def call(kernel, out_shape, *operands, in_specs, out_specs, scratch_shapes=(), flops):
    outs = out_shape if isinstance(out_shape, tuple) else (out_shape,)
    moved = sum(math.prod(o.shape) * o.dtype.itemsize for o in (*operands, *outs))
    return pl.pallas_call(
        kernel,
        out_shape=out_shape,
        in_specs=in_specs,
        out_specs=out_specs,
        scratch_shapes=scratch_shapes,
        compiler_params=pltpu.CompilerParams(vmem_limit_bytes=24 * MIB),
        cost_estimate=pl.CostEstimate(flops=flops, bytes_accessed=moved, transcendentals=0),
    )(*operands)


def shards(residual, queries, keys, values, grads, router, counts, rows, *, sizes):
    n_y, n_z, n_c, groups = sizes
    tok_dev, width = residual.shape
    slots = queries.shape[0]
    part = width // groups
    bf16, f32 = jnp.bfloat16, jnp.float32
    shape = jax.ShapeDtypeStruct
    packed = shape((groups, 4, slots, part), bf16)
    wide = shape((slots, width), bf16)
    dma = pltpu.SemaphoreType.DMA
    pin = functools.partial(pltpu.with_memory_space_constraint, memory_space=pltpu.HBM)
    router = router.reshape(1, width)
    counts, rows = counts.T, jnp.transpose(rows, (1, 2, 0))
    sent, picked, marks = call(
        functools.partial(prep_kernel, sizes=sizes),
        (pltpu.HBM(packed.shape, bf16), wide, shape((slots, LANES), f32)),
        *(pin(a) for a in (residual, queries, keys, values, grads, router, counts, rows)),
        in_specs=[HBM] * 8,
        out_specs=(HBM, VMEM, VMEM),
        scratch_shapes=[
            pltpu.VMEM((tok_dev, width), bf16),
            pltpu.VMEM((slots, width), bf16),
            pltpu.VMEM((3, slots, width), bf16),
            pltpu.VMEM((1, width), f32),
            pltpu.VMEM(counts.shape, jnp.int32),
            pltpu.VMEM(rows.shape[1:], jnp.int32),
            pltpu.VMEM((groups, slots, part), bf16),
            dma((8 + 4 * groups,)),
        ],
        flops=2 * slots * tok_dev * width,
    )

    def passed(array, distance):
        return lax.ppermute(array, "x", [(i, (i + distance) % groups) for i in range(groups)])

    got = lax.all_to_all(sent, "x", 0, 0)
    n = groups * slots
    mask, places = call(
        functools.partial(mask_kernel, sizes=sizes, tok_dev=tok_dev),
        (shape((n, n), f32), shape((8, LANES), f32)),
        counts, rows,
        in_specs=[VMEM] * 2, out_specs=(VMEM,) * 2, flops=10 * n * n,
    )
    attended, probs, dots = call(
        forward_kernel,
        (shape((n, part), bf16), shape((part // LANES, n, n), f32), shape((groups, 8, n), f32)),
        got, mask,
        in_specs=[VMEM] * 2, out_specs=(VMEM,) * 3, flops=4 * n * n * part,
    )
    dots = lax.all_to_all(dots, "x", 0, 0)
    back = call(
        backward_kernel, (pltpu.HBM((4, slots, part), bf16),) * groups, got, attended, probs,
        in_specs=[VMEM] * 3, out_specs=(HBM,) * groups,
        scratch_shapes=[pltpu.VMEM((groups, 3, slots, part), bf16), dma((2 * groups,))],
        flops=8 * n * n * part,
    )
    back = [back[0]] + [passed(back[d], d) for d in range(1, groups)]
    term = call(
        router_kernel, shape((ORDER[0][1](sizes), 1, width), f32), dots, picked, marks, pin(back[0]),
        in_specs=[VMEM] * 3 + [HBM], out_specs=VMEM, flops=4 * n * width,
    )
    total = jnp.sum(lax.all_to_all(term, ORDER[0][0], 0, 0), axis=0)
    for axes, size in ORDER[1:]:
        copies = jnp.broadcast_to(total[None], (size(sizes), 1, width))
        total = jnp.sum(lax.all_to_all(copies, axes, 0, 0), axis=0)
    block_out, d_queries, d_keys, d_values = call(
        finish_kernel,
        (shape((tok_dev, width), bf16), wide, wide, wide),
        *back, residual, picked, marks, places,
        in_specs=[VMEM] * (groups + 4),
        out_specs=(ANY,) * 4,
        scratch_shapes=[
            pltpu.VMEM((groups, tok_dev, part), bf16),
            pltpu.VMEM((3, groups, slots, part), bf16),
            dma((4 * groups,)),
        ],
        flops=2 * slots * tok_dev * width,
    )
    return block_out, d_queries, d_keys, d_values, total.reshape(width)


def split_dp(size):
    chips = size // CORES
    z = 2 ** (int(math.log2(chips)) // 2)
    return chips // z, z, CORES


def solution(mesh):
    sizes = (*split_dp(mesh.shape["dp"]), mesh.shape["seq"])
    fine = Mesh(mesh.devices.reshape(sizes), ("y", "z", "c", "x"))
    split = P(("y", "z", "c", "x"), None)
    return jax.shard_map(
        functools.partial(shards, sizes=sizes),
        mesh=fine,
        in_specs=(split,) * 5 + (P(),) * 3,
        out_specs=(split,) * 4 + (P(),),
        check_vma=False,
    )
```

time: 94.8 us -> 81.2 us (0.86)
  blocking collectives: 75.7 us -> 12 us
  starting transfers between devices: 0 us -> 38.8 us
  waiting for transfers between devices: 0 us -> 16.6 us
  local copies, waits for them, and re-layouts: 6.57 us -> 0.71 us
    all_to_all x5 -> x1, blocking collectives: 75.7 us -> 12 us  [shards(): total = jnp.sum(lax.all_to_all(copies, axes, 0, 0), axis=0)]
    all_to_all x0 -> x4, starting transfers between devices: none -> 29.5 us  [the longest x1 11.3 us: shards(): total = jnp.sum(lax.all_to_all(term, ORDER[0][0], 0, 0), axis=0)]
    all_to_all x0 -> x4, waiting for transfers between devices: none -> 16.6 us  [the longest x1 9.52 us: shards(): got = lax.all_to_all(sent, 'x', 0, 0)]
    ppermute x0 -> x3, starting transfers between devices: none -> 9.31 us  [passed(): lax.ppermute(array, 'x', [(i, (i + distance) % groups) for i in range(gro...]
    unnamed x16 -> x8, local copies, waits for them, and re-layouts: 6.56 us -> 0.03 us
    pallas_call x3 -> x6, Pallas kernels: 9.63 us -> 10.2 us  [call(): pl.pallas_call(kernel, out_shape=out_shape, in_specs=in_specs, out_specs=...]
  transfers between devices with their start and end apart: 0 -> 7, of which waited for: 0 -> 3; matrix products, arithmetic and copies ran while one was open for 0% -> 1% of each run, Pallas kernels for 0% -> 6%
where the time goes in v2:
time: 81.2 us; the launch traced here: 79.9 us
  starting transfers between devices  38.8 us (48%)
  waiting for transfers between devices  16.6 us (20%)
  blocking collectives  12 us (15%)
  Pallas kernels  10.2 us (13%)
    all_to_all x1, blocking collectives, shards(): total = jnp.sum(lax.all_to_all(copies, axes, 0, 0), axis=0)  12 us
    all_to_all x1, starting transfers between devices, shards(): total = jnp.sum(lax.all_to_all(term, ORDER[0][0], 0, 0), axis=0)  11.3 us
    pallas_call x6, Pallas kernels, call(): pl.pallas_call(kernel, out_shape=out_shape, in_specs=in_specs, out_specs=...  10.2 us
    all_to_all x1, starting transfers between devices, shards(): total = jnp.sum(lax.all_to_all(copies, axes, 0, 0), axis=0)  10 us
    all_to_all x1, waiting for transfers between devices, shards(): got = lax.all_to_all(sent, 'x', 0, 0)  9.52 us
    ppermute x3, starting transfers between devices, passed(): lax.ppermute(array, 'x', [(i, (i + distance) % groups) for i in range(gro...  9.31 us
    all_to_all x1, waiting for transfers between devices, shards(): total = jnp.sum(lax.all_to_all(copies, axes, 0, 0), axis=0)  5.48 us
    all_to_all x1, starting transfers between devices, shards(): got = lax.all_to_all(sent, 'x', 0, 0)  4.99 us
  transfers between devices with their start and end apart: 7, of which 3 were waited for; matrix products, arithmetic and copies ran while one was open for 1% of the time, Pallas kernels for 6%

profile of v2, /device:TPU:1, one launch (start us, length us, event | category | flops | bytes accessed | tf_op | source)
XLA Modules:
  0.0 79.9 jit_solution(8417589554344209981)
XLA Ops:
  0.6 2.8 %shard_map.119 = (bf16[4,4,64,512]{3,2,1,0:T(8,128)(2,1)}, bf16[64,2048]{1,0:T(8,128)(2,1)S(1)}, f32[64,128]{1,0:T(8,128)S(1)}) custom-call(bf16[256,2048]{1,0:T(8,128)(2,1)} %refs_4_.1, bf16[64,2048]{1,0:T(8,128)(2,1)} %queries.1, bf16[64,2048]{1,0:T(8,128)(2,1)} %keys.1, bf16[64,2048]{1,0:T(8,128)(2,1)} %values.1, bf16[64,2048]{1,0:T(8,128)(2,1)} %grads.1, ...), custom_call_target="tpu_custom_call" | custom-call | flops 67108864 | bytes 3581952 | tf_op jit(solution)/shard_map/pallas_call | solution.py:206
  3.5 0.0 copy-start.2
  3.5 0.0 copy-start.3
  3.5 5.0 %all-to-all-start = ((bf16[4,4,64,512]{3,2,1,0:T(8,128)(2,1)}), bf16[4,4,64,512]{3,2,1,0:T(8,128)(2,1)S(1)}, u32[]{:S(2)}, u32[]{:S(2)}) async-start(bf16[4,4,64,512]{3,2,1,0:T(8,128)(2,1)} %get-tuple-element.21), calls=%async_computation | async-start | bytes 2097152 | tf_op jit(solution)/shard_map/all_to_all | solution.py:252
  8.5 0.0 copy-done.2
  8.5 0.0 copy-done.3
  8.5 0.2 shard_map.120
  8.7 9.5 %all-to-all-done.got = bf16[4,4,64,512]{3,2,1,0:T(8,128)(2,1)S(1)} async-done(((bf16[4,4,64,512]{3,2,1,0:T(8,128)(2,1)}), bf16[4,4,64,512]{3,2,1,0:T(8,128)(2,1)S(1)}, u32[]{:S(2)}, u32[]{:S(2)}) %all-to-all-start) | async-done | bytes 1048608 | tf_op jit(solution)/shard_map/all_to_all | solution.py:252
  18.2 1.9 %shard_map.121 = (bf16[256,512]{1,0:T(8,128)(2,1)S(1)}, f32[4,256,256]{2,1,0:T(8,128)S(1)}, f32[4,8,256]{2,1,0:T(8,128)}) custom-call(bf16[4,4,64,512]{3,2,1,0:T(8,128)(2,1)S(1)} %all-to-all-done.got, f32[256,256]{1,0:T(8,128)S(1)} %get-tuple-element.22.mask), custom_call_target="tpu_custom_call" | custom-call | flops 134217728 | bytes 2654208 | tf_op jit(solution)/shard_map/pallas_call | solution.py:206
  20.2 3.3 %all-to-all-start.1 = ((f32[4,8,256]{2,1,0:T(8,128)}), f32[4,8,256]{2,1,0:T(8,128)S(1)}, u32[]{:S(2)}, u32[]{:S(2)}) async-start(f32[4,8,256]{2,1,0:T(8,128)} %get-tuple-element.36), calls=%async_computation.1 | async-start | bytes 65536 | tf_op jit(solution)/shard_map/all_to_all | solution.py:266
  23.4 2.7 %shard_map.122 = (bf16[4,64,512]{2,1,0:T(8,128)(2,1)}, bf16[4,64,512]{2,1,0:T(8,128)(2,1)}, bf16[4,64,512]{2,1,0:T(8,128)(2,1)}, bf16[4,64,512]{2,1,0:T(8,128)(2,1)}) custom-call(bf16[4,4,64,512]{3,2,1,0:T(8,128)(2,1)S(1)} %all-to-all-done.got, bf16[256,512]{1,0:T(8,128)(2,1)S(1)} %get-tuple-element.23.attended, f32[4,256,256]{2,1,0:T(8,128)S(1)} %get-tuple-element.24.probs), custom_call_target="tpu_custom_call" | custom-call | flops 268435456 | bytes 3407872 | tf_op jit(solution)/shard_map/pallas_call | solution.py:206
  26.1 0.0 copy-start
  26.1 1.6 %all-to-all-done.1.dots = f32[4,8,256]{2,1,0:T(8,128)S(1)} async-done(((f32[4,8,256]{2,1,0:T(8,128)}), f32[4,8,256]{2,1,0:T(8,128)S(1)}, u32[]{:S(2)}, u32[]{:S(2)}) %all-to-all-start.1) | async-done | bytes 32800 | tf_op jit(solution)/shard_map/all_to_all | solution.py:266
  27.7 0.9 %shard_map.124 = f32[8,1,2048]{2,1,0:T(1,128)} custom-call(f32[4,8,256]{2,1,0:T(8,128)S(1)} %all-to-all-done.1.dots, bf16[64,2048]{1,0:T(8,128)(2,1)S(1)} %get-tuple-element.29.refs_5_.picked, f32[64,128]{1,0:T(8,128)S(1)} %get-tuple-element.30.refs_6_.marks, bf16[4,64,512]{2,1,0:T(8,128)(2,1)} %get-tuple-element.25.refs_0_.after), custom_call_target="tpu_custom_call" | custom-call | flops 2097152 | bytes 655360 | tf_op jit(solution)/shard_map/pallas_call | solution.py:206
  28.5 11.3 %all-to-all-start.2 = ((f32[8,1,2048]{2,1,0:T(1,128)}), f32[8,1,2048]{2,1,0:T(1,128)S(1)}, u32[]{:S(2)}, u32[]{:S(2)}) async-start(f32[8,1,2048]{2,1,0:T(1,128)} %shard_map.124), calls=%async_computation.2 | async-start | bytes 131072 | tf_op jit(solution)/shard_map/all_to_all | solution.py:278
  39.8 2.2 %collective-permute-start = (bf16[4,64,512]{2,1,0:T(8,128)(2,1)}, bf16[4,64,512]{2,1,0:T(8,128)(2,1)S(1)}, u32[]{:S(2)}, u32[]{:S(2)}) collective-permute-start(bf16[4,64,512]{2,1,0:T(8,128)(2,1)} %get-tuple-element.26), channel_id=1, source_target_pairs={{0,1},{1,2},{2,3},{3,0},{4,5},{5,6},{6,7},{7,4},{8,9},{9,10},{10,1... | collective-permute-start | bytes 786440 | tf_op jit(solution)/shard_map/ppermute | solution.py:250
  42.0 3.9 %collective-permute-start.1 = (bf16[4,64,512]{2,1,0:T(8,128)(2,1)}, bf16[4,64,512]{2,1,0:T(8,128)(2,1)S(1)}, u32[]{:S(2)}, u32[]{:S(2)}) collective-permute-start(bf16[4,64,512]{2,1,0:T(8,128)(2,1)} %get-tuple-element.27), channel_id=1, source_target_pairs={{0,2},{1,3},{2,0},{3,1},{4,6},{5,7},{6,4},{7,5},{8,10},{9,11},{10,... | collective-permute-start | bytes 786440 | tf_op jit(solution)/shard_map/ppermute | solution.py:250
  45.9 0.0 copy-start.1
  45.9 3.2 %collective-permute-start.2 = (bf16[4,64,512]{2,1,0:T(8,128)(2,1)}, bf16[4,64,512]{2,1,0:T(8,128)(2,1)S(1)}, u32[]{:S(2)}, u32[]{:S(2)}) collective-permute-start(bf16[4,64,512]{2,1,0:T(8,128)(2,1)} %get-tuple-element.28), channel_id=1, source_target_pairs={{0,3},{1,0},{2,1},{3,2},{4,7},{5,4},{6,5},{7,6},{8,11},{9,8},{10,9... | collective-permute-start | bytes 786440 | tf_op jit(solution)/shard_map/ppermute | solution.py:250
  49.1 0.0 all-to-all-done.2
  49.2 0.1 reduce_sum.27
  49.3 12.0 %all_to_all.25 = f32[8,1,2048]{2,1,0:T(1,128)S(1)} all-to-all(f32[8,1,2048]{2,1,0:T(1,128)S(1)} %broadcast_in_dim.4), channel_id=1, replica_groups=mesh['y'=8,'z'=8,'c'=2,'x'=4] {'c','x'}, dimensions={0} | all-to-all | bytes 131072 | tf_op jit(solution)/shard_map/all_to_all | solution.py:281
  61.3 0.1 reduce_sum.28
  61.4 0.7 broadcast_in_dim.5
  62.0 10.0 %all-to-all-start.4 = ((f32[8,1,2048]{2,1,0:T(1,128)}), f32[8,1,2048]{2,1,0:T(1,128)S(1)}, u32[]{:S(2)}, u32[]{:S(2)}) async-start(f32[8,1,2048]{2,1,0:T(1,128)} %broadcast_in_dim.5), calls=%async_computation.4 | async-start | bytes 131072 | tf_op jit(solution)/shard_map/all_to_all | solution.py:281
  72.0 0.0 collective-permute-done.refs_1_
  72.1 0.0 collective-permute-done.1.refs_2_
  72.1 0.0 collective-permute-done.2.refs_3_
  72.1 0.0 copy-done
  72.1 0.0 copy-done.1
  72.1 1.7 %shard_map.123 = (bf16[256,2048]{1,0:T(8,128)(2,1)}, bf16[64,2048]{1,0:T(8,128)(2,1)}, bf16[64,2048]{1,0:T(8,128)(2,1)}, bf16[64,2048]{1,0:T(8,128)(2,1)}) custom-call(bf16[4,64,512]{2,1,0:T(8,128)(2,1)S(1)} %copy-done.1, bf16[4,64,512]{2,1,0:T(8,128)(2,1)S(1)} %collective-permute-done.refs_1_, bf16[4,64,512]{2,1,0:T(8,128)(2,1)S(1)} %collective-permute-done.1.refs_2_, ...), custom_call_target="tpu_custom_call" | custom-call | flops 67108864 | bytes 4231168 | tf_op jit(solution)/shard_map/pallas_call | solution.py:206
  73.8 5.5 %all-to-all-done.4 = f32[8,1,2048]{2,1,0:T(1,128)S(1)} async-done(((f32[8,1,2048]{2,1,0:T(1,128)}), f32[8,1,2048]{2,1,0:T(1,128)S(1)}, u32[]{:S(2)}, u32[]{:S(2)}) %all-to-all-start.4) | async-done | bytes 65568 | tf_op jit(solution)/shard_map/all_to_all | solution.py:281
  79.3 0.7 reduce_sum.29
  (1 shorter events, 0.0 us)
Async XLA Ops:
  3.5 5.0 %copy-start.2 = (s32[128,4,64]{0,2,1:T(8,128)S(1)}, s32[128,4,64]{0,2,1:T(8,128)}, u32[]{:S(2)}) copy-start(s32[128,4,64]{0,2,1:T(8,128)} %param.15) | copy-start | bytes 393220
  3.5 5.0 %copy-start.3 = (s32[128,4]{0,1:T(4,128)S(1)}, s32[128,4]{0,1:T(4,128)}, u32[]{:S(2)}) copy-start(s32[128,4]{0,1:T(4,128)} %param.14) | copy-start | bytes 6148
  3.5 14.7 %all-to-all-start = ((bf16[4,4,64,512]{3,2,1,0:T(8,128)(2,1)}), bf16[4,4,64,512]{3,2,1,0:T(8,128)(2,1)S(1)}, u32[]{:S(2)}, u32[]{:S(2)}) async-start(bf16[4,4,64,512]{3,2,1,0:T(8,128)(2,1)} %get-tuple-element.21), calls=%async_computation | async-start | bytes 2097152 | tf_op jit(solution)/shard_map/all_to_all | solution.py:252
  20.2 7.5 %all-to-all-start.1 = ((f32[4,8,256]{2,1,0:T(8,128)}), f32[4,8,256]{2,1,0:T(8,128)S(1)}, u32[]{:S(2)}, u32[]{:S(2)}) async-start(f32[4,8,256]{2,1,0:T(8,128)} %get-tuple-element.36), calls=%async_computation.1 | async-start | bytes 65536 | tf_op jit(solution)/shard_map/all_to_all | solution.py:266
  26.1 45.9 %copy-start = (bf16[256,2048]{1,0:T(8,128)(2,1)S(1)}, bf16[256,2048]{1,0:T(8,128)(2,1)}, u32[]{:S(2)}) copy-start(bf16[256,2048]{1,0:T(8,128)(2,1)} %refs_4_.1) | copy-start | bytes 3145732
  28.5 20.6 %all-to-all-start.2 = ((f32[8,1,2048]{2,1,0:T(1,128)}), f32[8,1,2048]{2,1,0:T(1,128)S(1)}, u32[]{:S(2)}, u32[]{:S(2)}) async-start(f32[8,1,2048]{2,1,0:T(1,128)} %shard_map.124), calls=%async_computation.2 | async-start | bytes 131072 | tf_op jit(solution)/shard_map/all_to_all | solution.py:278
  39.8 32.2 %collective-permute-start = (bf16[4,64,512]{2,1,0:T(8,128)(2,1)}, bf16[4,64,512]{2,1,0:T(8,128)(2,1)S(1)}, u32[]{:S(2)}, u32[]{:S(2)}) collective-permute-start(bf16[4,64,512]{2,1,0:T(8,128)(2,1)} %get-tuple-element.26), channel_id=1, source_target_pairs={{0,1},{1,2},{2,3},{3,0},{4,5},{5,6},{6,7},{7,4},{8,9},{9,10},{10,1... | collective-permute-start | bytes 786440 | tf_op jit(solution)/shard_map/ppermute | solution.py:250
  42.0 30.1 %collective-permute-start.1 = (bf16[4,64,512]{2,1,0:T(8,128)(2,1)}, bf16[4,64,512]{2,1,0:T(8,128)(2,1)S(1)}, u32[]{:S(2)}, u32[]{:S(2)}) collective-permute-start(bf16[4,64,512]{2,1,0:T(8,128)(2,1)} %get-tuple-element.27), channel_id=1, source_target_pairs={{0,2},{1,3},{2,0},{3,1},{4,6},{5,7},{6,4},{7,5},{8,10},{9,11},{10,... | collective-permute-start | bytes 786440 | tf_op jit(solution)/shard_map/ppermute | solution.py:250
  45.9 26.2 %copy-start.1 = (bf16[4,64,512]{2,1,0:T(8,128)(2,1)S(1)}, bf16[4,64,512]{2,1,0:T(8,128)(2,1)}, u32[]{:S(2)}) copy-start(bf16[4,64,512]{2,1,0:T(8,128)(2,1)} %get-tuple-element.25.refs_0_.after) | copy-start | bytes 786436
  45.9 26.1 %collective-permute-start.2 = (bf16[4,64,512]{2,1,0:T(8,128)(2,1)}, bf16[4,64,512]{2,1,0:T(8,128)(2,1)S(1)}, u32[]{:S(2)}, u32[]{:S(2)}) collective-permute-start(bf16[4,64,512]{2,1,0:T(8,128)(2,1)} %get-tuple-element.28), channel_id=1, source_target_pairs={{0,3},{1,0},{2,1},{3,2},{4,7},{5,4},{6,5},{7,6},{8,11},{9,8},{10,9... | collective-permute-start | bytes 786440 | tf_op jit(solution)/shard_map/ppermute | solution.py:250
  62.0 17.3 %all-to-all-start.4 = ((f32[8,1,2048]{2,1,0:T(1,128)}), f32[8,1,2048]{2,1,0:T(1,128)S(1)}, u32[]{:S(2)}, u32[]{:S(2)}) async-start(f32[8,1,2048]{2,1,0:T(1,128)} %broadcast_in_dim.5), calls=%async_computation.4 | async-start | bytes 131072 | tf_op jit(solution)/shard_map/all_to_all | solution.py:281

commit v3 on v2

--- a/solution.py
+++ b/solution.py
@@ -13,7 +13,7 @@
 LANES = 128
 CORES = 2
 MIB = 1024 * 1024
-ORDER = (("y", lambda s: s[0]), (("c", "x"), lambda s: s[2] * s[3]), ("z", lambda s: s[1]))
+ORDER = (("z", lambda s: s[1]), (("c", "x"), lambda s: s[2] * s[3]), ("y", lambda s: s[0]))
 VMEM = pl.BlockSpec(memory_space=pltpu.VMEM)
 ANY = pl.BlockSpec(memory_space=pl.ANY)
 HBM = pl.BlockSpec(memory_space=pltpu.HBM)
@@ -44,9 +44,12 @@
         return copy
 
     small = [fetch(rows.at[block_index], rows_v, 0), fetch(counts, counts_v, 1), fetch(router, router_v, 2)]
-    wide = [fetch(residual, residual_v, 3), fetch(grads, grads_v, 4)]
     pieces = [pl.ds(group * part, part) for group in range(groups)]
-    straight = [fetch(array, straight_v.at[i], 5 + i) for i, array in enumerate((queries, keys, values))]
+    wide = [fetch(residual.at[:, p], residual_v.at[:, p], 3 + i) for i, p in enumerate(pieces)]
+    base = 3 + groups
+    grads_copy = fetch(grads, grads_v, base)
+    straight = [fetch(array, straight_v.at[i], base + 1 + i) for i, array in enumerate((queries, keys, values))]
+    base += 4
     for copy in small:
         copy.wait()
     count = column(counts_v[...], dp_index)
@@ -55,28 +58,31 @@
     live = lax.broadcasted_iota(jnp.int32, (slots, 1), 0).astype(jnp.float32) < count
     token = lax.broadcasted_iota(jnp.int32, (slots, tokens), 1).astype(jnp.float32)
     pick = (column(rows_v[...], dp_index) == token).astype(jnp.bfloat16)
-    wide[0].wait()
-    x = jnp.dot(pick, residual_v[...], preferred_element_type=jnp.float32)
-    picked[...] = x.astype(jnp.bfloat16)
-    gate = jax.nn.sigmoid(jnp.sum(x * router_v[...], axis=1, keepdims=True))
+    logit = jnp.zeros((slots, part), jnp.float32)
+    for copy, p in zip(wide, pieces):
+        copy.wait()
+        x = jnp.dot(pick, residual_v[:, p], preferred_element_type=jnp.float32)
+        picked[:, p] = x.astype(jnp.bfloat16)
+        logit += x * router_v[:, p]
+    gate = jax.nn.sigmoid(jnp.sum(logit, axis=1, keepdims=True))
     lane = lax.broadcasted_iota(jnp.int32, marks.shape, 1)
     marks[...] = jnp.where(lane == 0, gate, live.astype(jnp.float32))
     copies = []
     for i, copy in enumerate(straight):
         copy.wait()
         for group in range(groups):
-            copies.append(fetch(straight_v.at[i, :, pieces[group]], sent.at[group, i], 8 + 4 * group + i))
-    wide[1].wait()
+            copies.append(fetch(straight_v.at[i, :, pieces[group]], sent.at[group, i], base + 4 * group + i))
+    grads_copy.wait()
     gate = jnp.where(live, gate, 0.0)
     for group in range(groups):
         columns = slice(group * part, (group + 1) * part)
         d_att_v[group] = (gate * grads_v[:, columns].astype(jnp.float32)).astype(jnp.bfloat16)
-        copies.append(fetch(d_att_v.at[group], sent.at[group, 3], 11 + 4 * group))
+        copies.append(fetch(d_att_v.at[group], sent.at[group, 3], base + 4 * group + 3))
     for copy in copies:
         copy.wait()
 
 
-def mask_kernel(counts, rows, mask, places, *, sizes, tok_dev):
+def places_kernel(counts, rows, places, *, sizes, tok_dev):
     blocks, slots, _ = rows.shape
     n = blocks * slots
     dp_index, block_index = sequence_index(sizes), lax.axis_index("x")
@@ -92,69 +98,68 @@
     down = lax.broadcasted_iota(jnp.int32, (n, n), 0)
     along = lax.broadcasted_iota(jnp.int32, (n, n), 1)
     seen = jnp.where(live, position, float(blocks * tok_dev))
-    seen = jnp.sum(jnp.where(down == along, seen, 0.0), axis=0, keepdims=True)
-    mask[...] = (seen <= position).astype(jnp.float32)
+    places[0:1, :] = jnp.sum(jnp.where(down == along, position, 0.0), axis=0, keepdims=True)
+    places[1:2, :] = jnp.sum(jnp.where(down == along, seen, 0.0), axis=0, keepdims=True)
     own = jnp.where(live & (block == block_index), row + 1.0, 0.0)
-    down = lax.broadcasted_iota(jnp.int32, (n, LANES), 0) % slots
-    along = lax.broadcasted_iota(jnp.int32, (n, LANES), 1)
-    own = jnp.sum(jnp.where(down == along, own, 0.0), axis=0, keepdims=True) - 1.0
-    places[...] = jnp.broadcast_to(own, places.shape)
-
-
-def forward_kernel(got, mask, attended, probs, dots):
+    own = jnp.sum(jnp.where(down % slots == along % slots, own, 0.0), axis=0, keepdims=True) - 1.0
+    places[2:3, :] = own
+
+
+def forward_kernel(got, places, probs, d_probs, dots):
     blocks, _, slots, part = got.shape
     n = blocks * slots
-    allowed = mask[...] > 0.0
+    down = lax.broadcasted_iota(jnp.int32, (n, n), 0)
+    along = lax.broadcasted_iota(jnp.int32, (n, n), 1)
+    seen = jnp.sum(jnp.where(down == along, places[1:2, :], 0.0), axis=1, keepdims=True)
+    allowed = seen <= places[0:1, :]
     inv_scale = 1.0 / math.sqrt(LANES)
     mm = functools.partial(lax.dot_general, preferred_element_type=jnp.float32)
-    dot = jnp.zeros((n, LANES), jnp.float32)
+    dot = jnp.zeros((1, n), jnp.float32)
     for head in range(part // LANES):
         columns = slice(head * LANES, (head + 1) * LANES)
         q, k, v, da = (got[:, i, :, columns].reshape(n, LANES) for i in range(4))
-        scores = mm(q, k, (((1,), (1,)), ((), ()))) * inv_scale
+        scores = mm(k, q, (((1,), (1,)), ((), ()))) * inv_scale
         scores = jnp.where(allowed, scores, -1e30)
-        e = jnp.exp(scores - jnp.max(scores, axis=1, keepdims=True))
-        weights = e * (1.0 / jnp.sum(e, axis=1, keepdims=True))
+        e = jnp.exp(scores - jnp.max(scores, axis=0, keepdims=True))
+        weights = e * (1.0 / jnp.sum(e, axis=0, keepdims=True))
         probs[head] = weights
-        att = mm(weights.astype(jnp.bfloat16), v, (((1,), (0,)), ((), ())))
-        attended[:, columns] = att.astype(jnp.bfloat16)
-        dot += att * da.astype(jnp.float32)
-    ones = jnp.ones((8, LANES), jnp.float32)
-    dot = mm(ones, dot, (((1,), (1,)), ((), ())), precision=lax.Precision.HIGHEST)
+        grad = mm(v, da, (((1,), (1,)), ((), ())))
+        d_probs[head] = grad
+        dot += jnp.sum(weights.astype(jnp.bfloat16).astype(jnp.float32) * grad, axis=0, keepdims=True)
     dots[...] = jnp.broadcast_to(dot[None], dots.shape)
 
 
-def backward_kernel(got, attended, probs, *refs):
+def backward_kernel(got, probs, d_probs, *refs):
     blocks, _, slots, part = got.shape
     *outs, held, sems = refs
     n = blocks * slots
     inv_scale = 1.0 / math.sqrt(LANES)
     mm = functools.partial(lax.dot_general, preferred_element_type=jnp.float32)
+    copies = []
     for head in range(part // LANES):
         columns = slice(head * LANES, (head + 1) * LANES)
         q, k, v, da = (got[:, i, :, columns].reshape(n, LANES) for i in range(4))
-        weights = probs[head]
-        d_probs = mm(da, v, (((1,), (1,)), ((), ())))
-        d_scores = weights * (d_probs - jnp.sum(weights * d_probs, axis=1, keepdims=True)) * inv_scale
-        d_scores = d_scores.astype(jnp.bfloat16)
-        dq = mm(d_scores, k, (((1,), (0,)), ((), ())))
-        dk = mm(d_scores, q, (((0,), (0,)), ((), ())))
-        dv = mm(weights.astype(jnp.bfloat16), da, (((0,), (0,)), ((), ())))
-        for i, value in enumerate((dq, dk, dv)):
+        weights, grad = probs[head], d_probs[head]
+        d_scores = weights * (grad - jnp.sum(weights * grad, axis=0, keepdims=True)) * inv_scale
+        d_scores, low = d_scores.astype(jnp.bfloat16), weights.astype(jnp.bfloat16)
+        att = mm(low, v, (((0,), (0,)), ((), ())))
+        dq = mm(d_scores, k, (((0,), (0,)), ((), ())))
+        dk = mm(d_scores, q, (((1,), (0,)), ((), ())))
+        dv = mm(low, da, (((1,), (0,)), ((), ())))
+        for i, value in enumerate((att, dq, dk, dv)):
             held[:, i, :, columns] = value.astype(jnp.bfloat16).reshape(blocks, slots, LANES)
-    copies = []
-    for distance, out in enumerate(outs):
-        block = lax.rem(lax.axis_index("x") + distance, blocks)
-        first = pl.multiple_of(block * slots, slots)
-        copies.append(pltpu.make_async_copy(attended.at[pl.ds(first, slots), :], out.at[0], sems.at[2 * distance]))
-        copies.append(pltpu.make_async_copy(held.at[block], out.at[pl.ds(1, 3)], sems.at[2 * distance + 1]))
+        if head % 2 == 1:
+            done = pl.ds((head - 1) * LANES, 2 * LANES)
+            for distance, out in enumerate(outs):
+                block = lax.rem(lax.axis_index("x") + distance, blocks)
+                copy = pltpu.make_async_copy(held.at[block, :, :, done], out.at[:, :, done], sems.at[len(copies)])
+                copy.start()
+                copies.append(copy)
     for copy in copies:
-        copy.start()
-    for copy in copies:
-        copy.wait()
-
-
-def router_kernel(dots, picked, marks, after, d_router):
+        copy.wait()
+
+
+def router_kernel(dots, picked, marks, after, d_router, tile):
     slots, width = picked.shape
     n = dots.shape[2]
     dot = jnp.sum(dots[...], axis=0)[0:1]
@@ -163,7 +168,9 @@
     dot = jnp.where(mine == lax.broadcasted_iota(jnp.int32, (slots, n), 1), dot, 0.0)
     d_logit = jnp.sum(dot, axis=1, keepdims=True) * (1.0 - marks[:, 0:1])
     term = jnp.sum(d_logit * picked[...].astype(jnp.float32), axis=0, keepdims=True)
-    d_router[...] = jnp.broadcast_to(term[None], d_router.shape)
+    for k in range(width // LANES):
+        tile[k : k + 1, :] = term[:, k * LANES : (k + 1) * LANES]
+    d_router[...] = jnp.broadcast_to(tile[...][None], d_router.shape)
 
 
 def finish_kernel(*refs):
@@ -173,7 +180,7 @@
     _, slots, part = got[0].shape
     tokens, width = residual.shape
     gate, live = marks[:, 0:1], marks[:, 1:2] > 0.0
-    own = places[0:1, :slots]
+    own = places[2:3, :slots]
     token = lax.broadcasted_iota(jnp.int32, (tokens, slots), 0).astype(jnp.float32)
     put = (token == own).astype(jnp.float32)
     hit = jnp.sum(put, axis=1, keepdims=True) > 0.0
@@ -241,7 +248,7 @@
             pltpu.VMEM(counts.shape, jnp.int32),
             pltpu.VMEM(rows.shape[1:], jnp.int32),
             pltpu.VMEM((groups, slots, part), bf16),
-            dma((8 + 4 * groups,)),
+            dma((7 + 5 * groups,)),
         ],
         flops=2 * slots * tok_dev * width,
     )
@@ -251,33 +258,34 @@
 
     got = lax.all_to_all(sent, "x", 0, 0)
     n = groups * slots
-    mask, places = call(
-        functools.partial(mask_kernel, sizes=sizes, tok_dev=tok_dev),
-        (shape((n, n), f32), shape((8, LANES), f32)),
-        counts, rows,
-        in_specs=[VMEM] * 2, out_specs=(VMEM,) * 2, flops=10 * n * n,
-    )
-    attended, probs, dots = call(
+    places = call(
+        functools.partial(places_kernel, sizes=sizes, tok_dev=tok_dev),
+        shape((8, n), f32), counts, rows,
+        in_specs=[VMEM] * 2, out_specs=VMEM, flops=10 * n * n,
+    )
+    square = shape((part // LANES, n, n), f32)
+    probs, d_probs, dots = call(
         forward_kernel,
-        (shape((n, part), bf16), shape((part // LANES, n, n), f32), shape((groups, 8, n), f32)),
-        got, mask,
+        (square, square, shape((groups, 8, n), f32)),
+        got, places,
         in_specs=[VMEM] * 2, out_specs=(VMEM,) * 3, flops=4 * n * n * part,
     )
     dots = lax.all_to_all(dots, "x", 0, 0)
     back = call(
-        backward_kernel, (pltpu.HBM((4, slots, part), bf16),) * groups, got, attended, probs,
+        backward_kernel, (pltpu.HBM((4, slots, part), bf16),) * groups, got, probs, d_probs,
         in_specs=[VMEM] * 3, out_specs=(HBM,) * groups,
-        scratch_shapes=[pltpu.VMEM((groups, 3, slots, part), bf16), dma((2 * groups,))],
+        scratch_shapes=[pltpu.VMEM((groups, 4, slots, part), bf16), dma((part // LANES // 2 * groups,))],
         flops=8 * n * n * part,
     )
     back = [back[0]] + [passed(back[d], d) for d in range(1, groups)]
     term = call(
-        router_kernel, shape((ORDER[0][1](sizes), 1, width), f32), dots, picked, marks, pin(back[0]),
-        in_specs=[VMEM] * 3 + [HBM], out_specs=VMEM, flops=4 * n * width,
+        router_kernel, shape((ORDER[0][1](sizes), width // LANES, LANES), f32), dots, picked, marks, pin(back[0]),
+        in_specs=[VMEM] * 3 + [HBM], out_specs=VMEM,
+        scratch_shapes=[pltpu.VMEM((width // LANES, LANES), f32)], flops=4 * n * width,
     )
     total = jnp.sum(lax.all_to_all(term, ORDER[0][0], 0, 0), axis=0)
     for axes, size in ORDER[1:]:
-        copies = jnp.broadcast_to(total[None], (size(sizes), 1, width))
+        copies = jnp.broadcast_to(total[None], (size(sizes), *total.shape))
         total = jnp.sum(lax.all_to_all(copies, axes, 0, 0), axis=0)
     block_out, d_queries, d_keys, d_values = call(
         finish_kernel,

time: 81.2 us -> 79.9 us (0.984)
  Pallas kernels: 10.2 us -> 8.78 us
  waiting for transfers between devices: 16.6 us -> 17.6 us
    all_to_all x1, starting transfers between devices: 11.3 us -> 14.5 us  [shards(): total = jnp.sum(lax.all_to_all(term, ORDER[0][0], 0, 0), axis=0)]
    all_to_all x1, starting transfers between devices: 10 us -> 6.82 us  [shards(): total = jnp.sum(lax.all_to_all(copies, axes, 0, 0), axis=0)]
    pallas_call x6, Pallas kernels: 10.2 us -> 8.78 us  [call(): pl.pallas_call(kernel, out_shape=out_shape, in_specs=in_specs, out_specs=...]
    all_to_all x1, waiting for transfers between devices: 1.55 us -> 2.58 us  [shards(): dots = lax.all_to_all(dots, 'x', 0, 0)]
  transfers between devices with their start and end apart: 7 -> 7, of which waited for: 3 -> 3; matrix products, arithmetic and copies ran while one was open for 1% -> 1% of each run, Pallas kernels for 6% -> 5%
where the time goes in v3:
time: 79.9 us; the launch traced here: 79.3 us
  starting transfers between devices  38.3 us (48%)
  waiting for transfers between devices  17.6 us (22%)
  blocking collectives  12.6 us (16%)
  Pallas kernels  8.78 us (11%)
  between operations  0.8 us (1%)
    all_to_all x1, starting transfers between devices, shards(): total = jnp.sum(lax.all_to_all(term, ORDER[0][0], 0, 0), axis=0)  14.5 us
    all_to_all x1, blocking collectives, shards(): total = jnp.sum(lax.all_to_all(copies, axes, 0, 0), axis=0)  12.6 us
    all_to_all x1, waiting for transfers between devices, shards(): got = lax.all_to_all(sent, 'x', 0, 0)  9.51 us
    pallas_call x6, Pallas kernels, call(): pl.pallas_call(kernel, out_shape=out_shape, in_specs=in_specs, out_specs=...  8.78 us
    ppermute x3, starting transfers between devices, passed(): lax.ppermute(array, 'x', [(i, (i + distance) % groups) for i in range(gro...  8.72 us
    all_to_all x1, starting transfers between devices, shards(): total = jnp.sum(lax.all_to_all(copies, axes, 0, 0), axis=0)  6.82 us
    all_to_all x1, waiting for transfers between devices, shards(): total = jnp.sum(lax.all_to_all(copies, axes, 0, 0), axis=0)  5.48 us
    all_to_all x1, starting transfers between devices, shards(): got = lax.all_to_all(sent, 'x', 0, 0)  4.99 us
  transfers between devices with their start and end apart: 7, of which 3 were waited for; matrix products, arithmetic and copies ran while one was open for 1% of the time, Pallas kernels for 5%

profile of v3, /device:TPU:1, one launch (start us, length us, event | category | flops | bytes accessed | tf_op | source)
XLA Modules:
  0.0 79.3 jit_solution(5631752692654937771)
XLA Ops:
  0.6 3.0 %shard_map.119 = (bf16[4,4,64,512]{3,2,1,0:T(8,128)(2,1)}, bf16[64,2048]{1,0:T(8,128)(2,1)S(1)}, f32[64,128]{1,0:T(8,128)S(1)}) custom-call(bf16[256,2048]{1,0:T(8,128)(2,1)} %refs_4_.1, bf16[64,2048]{1,0:T(8,128)(2,1)} %queries.1, bf16[64,2048]{1,0:T(8,128)(2,1)} %keys.1, bf16[64,2048]{1,0:T(8,128)(2,1)} %values.1, bf16[64,2048]{1,0:T(8,128)(2,1)} %grads.1, ...), custom_call_target="tpu_custom_call" | custom-call | flops 67108864 | bytes 3581952 | tf_op jit(solution)/shard_map/pallas_call | solution.py:213
  3.6 0.0 copy-start.2
  3.6 0.0 copy-start.3
  3.6 5.0 %all-to-all-start = ((bf16[4,4,64,512]{3,2,1,0:T(8,128)(2,1)}), bf16[4,4,64,512]{3,2,1,0:T(8,128)(2,1)S(1)}, u32[]{:S(2)}, u32[]{:S(2)}) async-start(bf16[4,4,64,512]{3,2,1,0:T(8,128)(2,1)} %get-tuple-element.19), calls=%async_computation | async-start | bytes 2097152 | tf_op jit(solution)/shard_map/all_to_all | solution.py:259
  8.6 0.0 copy-done.2
  8.6 0.0 copy-done.3
  8.6 0.2 shard_map.120.places.refs_7_
  8.9 9.5 %all-to-all-done.got = bf16[4,4,64,512]{3,2,1,0:T(8,128)(2,1)S(1)} async-done(((bf16[4,4,64,512]{3,2,1,0:T(8,128)(2,1)}), bf16[4,4,64,512]{3,2,1,0:T(8,128)(2,1)S(1)}, u32[]{:S(2)}, u32[]{:S(2)}) %all-to-all-start) | async-done | bytes 1048608 | tf_op jit(solution)/shard_map/all_to_all | solution.py:259
  18.4 1.4 %shard_map.121 = (f32[4,256,256]{2,1,0:T(8,128)S(1)}, f32[4,256,256]{2,1,0:T(8,128)S(1)}, f32[4,8,256]{2,1,0:T(8,128)}) custom-call(bf16[4,4,64,512]{3,2,1,0:T(8,128)(2,1)S(1)} %all-to-all-done.got, f32[8,256]{1,0:T(8,128)S(1)} %shard_map.120.places.refs_7_), custom_call_target="tpu_custom_call" | custom-call | flops 134217728 | bytes 3186688 | tf_op jit(solution)/shard_map/pallas_call | solution.py:213
  19.7 3.3 %all-to-all-start.1 = ((f32[4,8,256]{2,1,0:T(8,128)}), f32[4,8,256]{2,1,0:T(8,128)S(1)}, u32[]{:S(2)}, u32[]{:S(2)}) async-start(f32[4,8,256]{2,1,0:T(8,128)} %get-tuple-element.32), calls=%async_computation.1 | async-start | bytes 65536 | tf_op jit(solution)/shard_map/all_to_all | solution.py:273
  23.0 1.7 %shard_map.122 = (bf16[4,64,512]{2,1,0:T(8,128)(2,1)}, bf16[4,64,512]{2,1,0:T(8,128)(2,1)}, bf16[4,64,512]{2,1,0:T(8,128)(2,1)}, bf16[4,64,512]{2,1,0:T(8,128)(2,1)}) custom-call(bf16[4,4,64,512]{3,2,1,0:T(8,128)(2,1)S(1)} %all-to-all-done.got, f32[4,256,256]{2,1,0:T(8,128)S(1)} %get-tuple-element.20.probs, f32[4,256,256]{2,1,0:T(8,128)S(1)} %get-tuple-element.21.d_probs), custom_call_target="tpu_custom_call" | custom-call | flops 268435456 | bytes 4194304 | tf_op jit(solution)/shard_map/pallas_call | solution.py:213
  24.7 0.0 copy-start
  24.7 2.6 %all-to-all-done.1.dots = f32[4,8,256]{2,1,0:T(8,128)S(1)} async-done(((f32[4,8,256]{2,1,0:T(8,128)}), f32[4,8,256]{2,1,0:T(8,128)S(1)}, u32[]{:S(2)}, u32[]{:S(2)}) %all-to-all-start.1) | async-done | bytes 32800 | tf_op jit(solution)/shard_map/all_to_all | solution.py:273
  27.3 0.9 %shard_map.124 = f32[8,16,128]{2,1,0:T(8,128)} custom-call(f32[4,8,256]{2,1,0:T(8,128)S(1)} %all-to-all-done.1.dots, bf16[64,2048]{1,0:T(8,128)(2,1)S(1)} %get-tuple-element.26.refs_5_.picked, f32[64,128]{1,0:T(8,128)S(1)} %get-tuple-element.27.refs_6_.marks, bf16[4,64,512]{2,1,0:T(8,128)(2,1)} %get-tuple-element.22.refs_0_.after), custom_call_target="tpu_custom_call" | custom-call | flops 2097152 | bytes 655360 | tf_op jit(solution)/shard_map/pallas_call | solution.py:213
  28.1 14.5 %all-to-all-start.2 = ((f32[8,16,128]{2,1,0:T(8,128)}), f32[8,16,128]{2,1,0:T(8,128)S(1)}, u32[]{:S(2)}, u32[]{:S(2)}) async-start(f32[8,16,128]{2,1,0:T(8,128)} %shard_map.124), calls=%async_computation.2 | async-start | bytes 131072 | tf_op jit(solution)/shard_map/all_to_all | solution.py:286
  42.6 2.2 %collective-permute-start = (bf16[4,64,512]{2,1,0:T(8,128)(2,1)}, bf16[4,64,512]{2,1,0:T(8,128)(2,1)S(1)}, u32[]{:S(2)}, u32[]{:S(2)}) collective-permute-start(bf16[4,64,512]{2,1,0:T(8,128)(2,1)} %get-tuple-element.23), channel_id=1, source_target_pairs={{0,1},{1,2},{2,3},{3,0},{4,5},{5,6},{6,7},{7,4},{8,9},{9,10},{10,1... | collective-permute-start | bytes 786440 | tf_op jit(solution)/shard_map/ppermute | solution.py:257
  44.8 3.7 %collective-permute-start.1 = (bf16[4,64,512]{2,1,0:T(8,128)(2,1)}, bf16[4,64,512]{2,1,0:T(8,128)(2,1)S(1)}, u32[]{:S(2)}, u32[]{:S(2)}) collective-permute-start(bf16[4,64,512]{2,1,0:T(8,128)(2,1)} %get-tuple-element.24), channel_id=1, source_target_pairs={{0,2},{1,3},{2,0},{3,1},{4,6},{5,7},{6,4},{7,5},{8,10},{9,11},{10,... | collective-permute-start | bytes 786440 | tf_op jit(solution)/shard_map/ppermute | solution.py:257
  48.5 0.0 copy-start.1
  48.5 2.8 %collective-permute-start.2 = (bf16[4,64,512]{2,1,0:T(8,128)(2,1)}, bf16[4,64,512]{2,1,0:T(8,128)(2,1)S(1)}, u32[]{:S(2)}, u32[]{:S(2)}) collective-permute-start(bf16[4,64,512]{2,1,0:T(8,128)(2,1)} %get-tuple-element.25), channel_id=1, source_target_pairs={{0,3},{1,0},{2,1},{3,2},{4,7},{5,4},{6,5},{7,6},{8,11},{9,8},{10,9... | collective-permute-start | bytes 786440 | tf_op jit(solution)/shard_map/ppermute | solution.py:257
  51.3 0.0 all-to-all-done.2
  51.4 12.6 %all_to_all.25 = f32[8,16,128]{2,1,0:T(8,128)S(1)} all-to-all(f32[8,16,128]{2,1,0:T(8,128)S(1)} %broadcast_in_dim.4), channel_id=1, replica_groups=mesh['y'=8,'z'=8,'c'=2,'x'=4] {'c','x'}, dimensions={0} | all-to-all | bytes 131072 | tf_op jit(solution)/shard_map/all_to_all | solution.py:289
  64.0 0.6 broadcast_in_dim.5
  64.7 6.8 %all-to-all-start.4 = ((f32[8,16,128]{2,1,0:T(8,128)}), f32[8,16,128]{2,1,0:T(8,128)S(1)}, u32[]{:S(2)}, u32[]{:S(2)}) async-start(f32[8,16,128]{2,1,0:T(8,128)} %broadcast_in_dim.5), calls=%async_computation.4 | async-start | bytes 131072 | tf_op jit(solution)/shard_map/all_to_all | solution.py:289
  71.5 0.0 collective-permute-done.refs_1_
  71.5 0.0 collective-permute-done.1.refs_2_
  71.5 0.0 collective-permute-done.2.refs_3_
  71.5 0.0 copy-done
  71.5 0.0 copy-done.1
  71.5 1.7 %shard_map.123 = (bf16[256,2048]{1,0:T(8,128)(2,1)}, bf16[64,2048]{1,0:T(8,128)(2,1)}, bf16[64,2048]{1,0:T(8,128)(2,1)}, bf16[64,2048]{1,0:T(8,128)(2,1)}) custom-call(bf16[4,64,512]{2,1,0:T(8,128)(2,1)S(1)} %copy-done.1, bf16[4,64,512]{2,1,0:T(8,128)(2,1)S(1)} %collective-permute-done.refs_1_, bf16[4,64,512]{2,1,0:T(8,128)(2,1)S(1)} %collective-permute-done.1.refs_2_, ...), custom_call_target="tpu_custom_call" | custom-call | flops 67108864 | bytes 4235264 | tf_op jit(solution)/shard_map/pallas_call | solution.py:213
  73.2 5.5 %all-to-all-done.4 = f32[8,16,128]{2,1,0:T(8,128)S(1)} async-done(((f32[8,16,128]{2,1,0:T(8,128)}), f32[8,16,128]{2,1,0:T(8,128)S(1)}, u32[]{:S(2)}, u32[]{:S(2)}) %all-to-all-start.4) | async-done | bytes 65568 | tf_op jit(solution)/shard_map/all_to_all | solution.py:289
  78.7 0.6 reduce_sum.29
  (3 shorter events, 0.0 us)
Async XLA Ops:
  3.6 5.0 %copy-start.2 = (s32[128,4,64]{0,2,1:T(8,128)S(1)}, s32[128,4,64]{0,2,1:T(8,128)}, u32[]{:S(2)}) copy-start(s32[128,4,64]{0,2,1:T(8,128)} %param.15) | copy-start | bytes 393220
  3.6 5.0 %copy-start.3 = (s32[128,4]{0,1:T(4,128)S(1)}, s32[128,4]{0,1:T(4,128)}, u32[]{:S(2)}) copy-start(s32[128,4]{0,1:T(4,128)} %param.14) | copy-start | bytes 6148
  3.6 14.7 %all-to-all-start = ((bf16[4,4,64,512]{3,2,1,0:T(8,128)(2,1)}), bf16[4,4,64,512]{3,2,1,0:T(8,128)(2,1)S(1)}, u32[]{:S(2)}, u32[]{:S(2)}) async-start(bf16[4,4,64,512]{3,2,1,0:T(8,128)(2,1)} %get-tuple-element.19), calls=%async_computation | async-start | bytes 2097152 | tf_op jit(solution)/shard_map/all_to_all | solution.py:259
  19.7 7.5 %all-to-all-start.1 = ((f32[4,8,256]{2,1,0:T(8,128)}), f32[4,8,256]{2,1,0:T(8,128)S(1)}, u32[]{:S(2)}, u32[]{:S(2)}) async-start(f32[4,8,256]{2,1,0:T(8,128)} %get-tuple-element.32), calls=%async_computation.1 | async-start | bytes 65536 | tf_op jit(solution)/shard_map/all_to_all | solution.py:273
  24.7 46.8 %copy-start = (bf16[256,2048]{1,0:T(8,128)(2,1)S(1)}, bf16[256,2048]{1,0:T(8,128)(2,1)}, u32[]{:S(2)}) copy-start(bf16[256,2048]{1,0:T(8,128)(2,1)} %refs_4_.1) | copy-start | bytes 3145732
  28.1 23.2 %all-to-all-start.2 = ((f32[8,16,128]{2,1,0:T(8,128)}), f32[8,16,128]{2,1,0:T(8,128)S(1)}, u32[]{:S(2)}, u32[]{:S(2)}) async-start(f32[8,16,128]{2,1,0:T(8,128)} %shard_map.124), calls=%async_computation.2 | async-start | bytes 131072 | tf_op jit(solution)/shard_map/all_to_all | solution.py:286
  42.6 28.9 %collective-permute-start = (bf16[4,64,512]{2,1,0:T(8,128)(2,1)}, bf16[4,64,512]{2,1,0:T(8,128)(2,1)S(1)}, u32[]{:S(2)}, u32[]{:S(2)}) collective-permute-start(bf16[4,64,512]{2,1,0:T(8,128)(2,1)} %get-tuple-element.23), channel_id=1, source_target_pairs={{0,1},{1,2},{2,3},{3,0},{4,5},{5,6},{6,7},{7,4},{8,9},{9,10},{10,1... | collective-permute-start | bytes 786440 | tf_op jit(solution)/shard_map/ppermute | solution.py:257
  44.8 26.7 %collective-permute-start.1 = (bf16[4,64,512]{2,1,0:T(8,128)(2,1)}, bf16[4,64,512]{2,1,0:T(8,128)(2,1)S(1)}, u32[]{:S(2)}, u32[]{:S(2)}) collective-permute-start(bf16[4,64,512]{2,1,0:T(8,128)(2,1)} %get-tuple-element.24), channel_id=1, source_target_pairs={{0,2},{1,3},{2,0},{3,1},{4,6},{5,7},{6,4},{7,5},{8,10},{9,11},{10,... | collective-permute-start | bytes 786440 | tf_op jit(solution)/shard_map/ppermute | solution.py:257
  48.5 23.0 %copy-start.1 = (bf16[4,64,512]{2,1,0:T(8,128)(2,1)S(1)}, bf16[4,64,512]{2,1,0:T(8,128)(2,1)}, u32[]{:S(2)}) copy-start(bf16[4,64,512]{2,1,0:T(8,128)(2,1)} %get-tuple-element.22.refs_0_.after) | copy-start | bytes 786436
  48.5 23.0 %collective-permute-start.2 = (bf16[4,64,512]{2,1,0:T(8,128)(2,1)}, bf16[4,64,512]{2,1,0:T(8,128)(2,1)S(1)}, u32[]{:S(2)}, u32[]{:S(2)}) collective-permute-start(bf16[4,64,512]{2,1,0:T(8,128)(2,1)} %get-tuple-element.25), channel_id=1, source_target_pairs={{0,3},{1,0},{2,1},{3,2},{4,7},{5,4},{6,5},{7,6},{8,11},{9,8},{10,9... | collective-permute-start | bytes 786440 | tf_op jit(solution)/shard_map/ppermute | solution.py:257
  64.7 14.1 %all-to-all-start.4 = ((f32[8,16,128]{2,1,0:T(8,128)}), f32[8,16,128]{2,1,0:T(8,128)S(1)}, u32[]{:S(2)}, u32[]{:S(2)}) async-start(f32[8,16,128]{2,1,0:T(8,128)} %broadcast_in_dim.5), calls=%async_computation.4 | async-start | bytes 131072 | tf_op jit(solution)/shard_map/all_to_all | solution.py:289

commit v4 on v3

--- a/solution.py
+++ b/solution.py
@@ -45,10 +45,10 @@
 
     small = [fetch(rows.at[block_index], rows_v, 0), fetch(counts, counts_v, 1), fetch(router, router_v, 2)]
     pieces = [pl.ds(group * part, part) for group in range(groups)]
+    base = 3 + groups
+    straight = [fetch(array, straight_v.at[i], base + 1 + i) for i, array in enumerate((queries, keys, values))]
     wide = [fetch(residual.at[:, p], residual_v.at[:, p], 3 + i) for i, p in enumerate(pieces)]
-    base = 3 + groups
     grads_copy = fetch(grads, grads_v, base)
-    straight = [fetch(array, straight_v.at[i], base + 1 + i) for i, array in enumerate((queries, keys, values))]
     base += 4
     for copy in small:
         copy.wait()
@@ -58,6 +58,11 @@
     live = lax.broadcasted_iota(jnp.int32, (slots, 1), 0).astype(jnp.float32) < count
     token = lax.broadcasted_iota(jnp.int32, (slots, tokens), 1).astype(jnp.float32)
     pick = (column(rows_v[...], dp_index) == token).astype(jnp.bfloat16)
+    copies = []
+    for i, copy in enumerate(straight):
+        copy.wait()
+        for group in range(groups):
+            copies.append(fetch(straight_v.at[i, :, pieces[group]], sent.at[group, i], base + 4 * group + i))
     logit = jnp.zeros((slots, part), jnp.float32)
     for copy, p in zip(wide, pieces):
         copy.wait()
@@ -67,11 +72,6 @@
     gate = jax.nn.sigmoid(jnp.sum(logit, axis=1, keepdims=True))
     lane = lax.broadcasted_iota(jnp.int32, marks.shape, 1)
     marks[...] = jnp.where(lane == 0, gate, live.astype(jnp.float32))
-    copies = []
-    for i, copy in enumerate(straight):
-        copy.wait()
-        for group in range(groups):
-            copies.append(fetch(straight_v.at[i, :, pieces[group]], sent.at[group, i], base + 4 * group + i))
     grads_copy.wait()
     gate = jnp.where(live, gate, 0.0)
     for group in range(groups):

time: 79.9 us -> 79.9 us (level)
  no operation moved by 1% of the time
where the time goes in v4:
time: 79.9 us; the launch traced here: 79.3 us
  starting transfers between devices  38.3 us (48%)
  waiting for transfers between devices  17.6 us (22%)
  blocking collectives  12.6 us (16%)
  Pallas kernels  8.76 us (11%)
  between operations  0.8 us (1%)
    all_to_all x1, starting transfers between devices, shards(): total = jnp.sum(lax.all_to_all(term, ORDER[0][0], 0, 0), axis=0)  14.5 us
    all_to_all x1, blocking collectives, shards(): total = jnp.sum(lax.all_to_all(copies, axes, 0, 0), axis=0)  12.6 us
    all_to_all x1, waiting for transfers between devices, shards(): got = lax.all_to_all(sent, 'x', 0, 0)  9.51 us
    pallas_call x6, Pallas kernels, call(): pl.pallas_call(kernel, out_shape=out_shape, in_specs=in_specs, out_specs=...  8.76 us
    ppermute x3, starting transfers between devices, passed(): lax.ppermute(array, 'x', [(i, (i + distance) % groups) for i in range(gro...  8.72 us
    all_to_all x1, starting transfers between devices, shards(): total = jnp.sum(lax.all_to_all(copies, axes, 0, 0), axis=0)  6.82 us
    all_to_all x1, waiting for transfers between devices, shards(): total = jnp.sum(lax.all_to_all(copies, axes, 0, 0), axis=0)  5.49 us
    all_to_all x1, starting transfers between devices, shards(): got = lax.all_to_all(sent, 'x', 0, 0)  4.99 us
  transfers between devices with their start and end apart: 7, of which 3 were waited for; matrix products, arithmetic and copies ran while one was open for 1% of the time, Pallas kernels for 5%

profile of v4, /device:TPU:1, one launch (start us, length us, event | category | flops | bytes accessed | tf_op | source)
XLA Modules:
  0.0 79.3 jit_solution(15966875633668847773)
XLA Ops:
  0.6 3.0 %shard_map.119 = (bf16[4,4,64,512]{3,2,1,0:T(8,128)(2,1)}, bf16[64,2048]{1,0:T(8,128)(2,1)S(1)}, f32[64,128]{1,0:T(8,128)S(1)}) custom-call(bf16[256,2048]{1,0:T(8,128)(2,1)} %refs_4_.1, bf16[64,2048]{1,0:T(8,128)(2,1)} %queries.1, bf16[64,2048]{1,0:T(8,128)(2,1)} %keys.1, bf16[64,2048]{1,0:T(8,128)(2,1)} %values.1, bf16[64,2048]{1,0:T(8,128)(2,1)} %grads.1, ...), custom_call_target="tpu_custom_call" | custom-call | flops 67108864 | bytes 3581952 | tf_op jit(solution)/shard_map/pallas_call | solution.py:213
  3.6 0.0 copy-start.2
  3.6 0.0 copy-start.3
  3.6 5.0 %all-to-all-start = ((bf16[4,4,64,512]{3,2,1,0:T(8,128)(2,1)}), bf16[4,4,64,512]{3,2,1,0:T(8,128)(2,1)S(1)}, u32[]{:S(2)}, u32[]{:S(2)}) async-start(bf16[4,4,64,512]{3,2,1,0:T(8,128)(2,1)} %get-tuple-element.19), calls=%async_computation | async-start | bytes 2097152 | tf_op jit(solution)/shard_map/all_to_all | solution.py:259
  8.6 0.0 copy-done.2
  8.6 0.0 copy-done.3
  8.6 0.2 shard_map.120.places.refs_7_
  8.8 9.5 %all-to-all-done.got = bf16[4,4,64,512]{3,2,1,0:T(8,128)(2,1)S(1)} async-done(((bf16[4,4,64,512]{3,2,1,0:T(8,128)(2,1)}), bf16[4,4,64,512]{3,2,1,0:T(8,128)(2,1)S(1)}, u32[]{:S(2)}, u32[]{:S(2)}) %all-to-all-start) | async-done | bytes 1048608 | tf_op jit(solution)/shard_map/all_to_all | solution.py:259
  18.4 1.4 %shard_map.121 = (f32[4,256,256]{2,1,0:T(8,128)S(1)}, f32[4,256,256]{2,1,0:T(8,128)S(1)}, f32[4,8,256]{2,1,0:T(8,128)}) custom-call(bf16[4,4,64,512]{3,2,1,0:T(8,128)(2,1)S(1)} %all-to-all-done.got, f32[8,256]{1,0:T(8,128)S(1)} %shard_map.120.places.refs_7_), custom_call_target="tpu_custom_call" | custom-call | flops 134217728 | bytes 3186688 | tf_op jit(solution)/shard_map/pallas_call | solution.py:213
  19.7 3.3 %all-to-all-start.1 = ((f32[4,8,256]{2,1,0:T(8,128)}), f32[4,8,256]{2,1,0:T(8,128)S(1)}, u32[]{:S(2)}, u32[]{:S(2)}) async-start(f32[4,8,256]{2,1,0:T(8,128)} %get-tuple-element.32), calls=%async_computation.1 | async-start | bytes 65536 | tf_op jit(solution)/shard_map/all_to_all | solution.py:273
  23.0 1.7 %shard_map.122 = (bf16[4,64,512]{2,1,0:T(8,128)(2,1)}, bf16[4,64,512]{2,1,0:T(8,128)(2,1)}, bf16[4,64,512]{2,1,0:T(8,128)(2,1)}, bf16[4,64,512]{2,1,0:T(8,128)(2,1)}) custom-call(bf16[4,4,64,512]{3,2,1,0:T(8,128)(2,1)S(1)} %all-to-all-done.got, f32[4,256,256]{2,1,0:T(8,128)S(1)} %get-tuple-element.20.probs, f32[4,256,256]{2,1,0:T(8,128)S(1)} %get-tuple-element.21.d_probs), custom_call_target="tpu_custom_call" | custom-call | flops 268435456 | bytes 4194304 | tf_op jit(solution)/shard_map/pallas_call | solution.py:213
  24.7 0.0 copy-start
  24.7 2.6 %all-to-all-done.1.dots = f32[4,8,256]{2,1,0:T(8,128)S(1)} async-done(((f32[4,8,256]{2,1,0:T(8,128)}), f32[4,8,256]{2,1,0:T(8,128)S(1)}, u32[]{:S(2)}, u32[]{:S(2)}) %all-to-all-start.1) | async-done | bytes 32800 | tf_op jit(solution)/shard_map/all_to_all | solution.py:273
  27.3 0.9 %shard_map.124 = f32[8,16,128]{2,1,0:T(8,128)} custom-call(f32[4,8,256]{2,1,0:T(8,128)S(1)} %all-to-all-done.1.dots, bf16[64,2048]{1,0:T(8,128)(2,1)S(1)} %get-tuple-element.26.refs_5_.picked, f32[64,128]{1,0:T(8,128)S(1)} %get-tuple-element.27.refs_6_.marks, bf16[4,64,512]{2,1,0:T(8,128)(2,1)} %get-tuple-element.22.refs_0_.after), custom_call_target="tpu_custom_call" | custom-call | flops 2097152 | bytes 655360 | tf_op jit(solution)/shard_map/pallas_call | solution.py:213
  28.1 14.5 %all-to-all-start.2 = ((f32[8,16,128]{2,1,0:T(8,128)}), f32[8,16,128]{2,1,0:T(8,128)S(1)}, u32[]{:S(2)}, u32[]{:S(2)}) async-start(f32[8,16,128]{2,1,0:T(8,128)} %shard_map.124), calls=%async_computation.2 | async-start | bytes 131072 | tf_op jit(solution)/shard_map/all_to_all | solution.py:286
  42.6 2.2 %collective-permute-start = (bf16[4,64,512]{2,1,0:T(8,128)(2,1)}, bf16[4,64,512]{2,1,0:T(8,128)(2,1)S(1)}, u32[]{:S(2)}, u32[]{:S(2)}) collective-permute-start(bf16[4,64,512]{2,1,0:T(8,128)(2,1)} %get-tuple-element.23), channel_id=1, source_target_pairs={{0,1},{1,2},{2,3},{3,0},{4,5},{5,6},{6,7},{7,4},{8,9},{9,10},{10,1... | collective-permute-start | bytes 786440 | tf_op jit(solution)/shard_map/ppermute | solution.py:257
  44.8 3.7 %collective-permute-start.1 = (bf16[4,64,512]{2,1,0:T(8,128)(2,1)}, bf16[4,64,512]{2,1,0:T(8,128)(2,1)S(1)}, u32[]{:S(2)}, u32[]{:S(2)}) collective-permute-start(bf16[4,64,512]{2,1,0:T(8,128)(2,1)} %get-tuple-element.24), channel_id=1, source_target_pairs={{0,2},{1,3},{2,0},{3,1},{4,6},{5,7},{6,4},{7,5},{8,10},{9,11},{10,... | collective-permute-start | bytes 786440 | tf_op jit(solution)/shard_map/ppermute | solution.py:257
  48.5 0.0 copy-start.1
  48.5 2.8 %collective-permute-start.2 = (bf16[4,64,512]{2,1,0:T(8,128)(2,1)}, bf16[4,64,512]{2,1,0:T(8,128)(2,1)S(1)}, u32[]{:S(2)}, u32[]{:S(2)}) collective-permute-start(bf16[4,64,512]{2,1,0:T(8,128)(2,1)} %get-tuple-element.25), channel_id=1, source_target_pairs={{0,3},{1,0},{2,1},{3,2},{4,7},{5,4},{6,5},{7,6},{8,11},{9,8},{10,9... | collective-permute-start | bytes 786440 | tf_op jit(solution)/shard_map/ppermute | solution.py:257
  51.3 0.0 all-to-all-done.2
  51.4 12.6 %all_to_all.25 = f32[8,16,128]{2,1,0:T(8,128)S(1)} all-to-all(f32[8,16,128]{2,1,0:T(8,128)S(1)} %broadcast_in_dim.4), channel_id=1, replica_groups=mesh['y'=8,'z'=8,'c'=2,'x'=4] {'c','x'}, dimensions={0} | all-to-all | bytes 131072 | tf_op jit(solution)/shard_map/all_to_all | solution.py:289
  64.0 0.6 broadcast_in_dim.5
  64.7 6.8 %all-to-all-start.4 = ((f32[8,16,128]{2,1,0:T(8,128)}), f32[8,16,128]{2,1,0:T(8,128)S(1)}, u32[]{:S(2)}, u32[]{:S(2)}) async-start(f32[8,16,128]{2,1,0:T(8,128)} %broadcast_in_dim.5), calls=%async_computation.4 | async-start | bytes 131072 | tf_op jit(solution)/shard_map/all_to_all | solution.py:289
  71.5 0.0 collective-permute-done.refs_1_
  71.5 0.0 collective-permute-done.1.refs_2_
  71.5 0.0 collective-permute-done.2.refs_3_
  71.5 0.0 copy-done
  71.5 0.0 copy-done.1
  71.5 1.7 %shard_map.123 = (bf16[256,2048]{1,0:T(8,128)(2,1)}, bf16[64,2048]{1,0:T(8,128)(2,1)}, bf16[64,2048]{1,0:T(8,128)(2,1)}, bf16[64,2048]{1,0:T(8,128)(2,1)}) custom-call(bf16[4,64,512]{2,1,0:T(8,128)(2,1)S(1)} %copy-done.1, bf16[4,64,512]{2,1,0:T(8,128)(2,1)S(1)} %collective-permute-done.refs_1_, bf16[4,64,512]{2,1,0:T(8,128)(2,1)S(1)} %collective-permute-done.1.refs_2_, ...), custom_call_target="tpu_custom_call" | custom-call | flops 67108864 | bytes 4235264 | tf_op jit(solution)/shard_map/pallas_call | solution.py:213
  73.2 5.5 %all-to-all-done.4 = f32[8,16,128]{2,1,0:T(8,128)S(1)} async-done(((f32[8,16,128]{2,1,0:T(8,128)}), f32[8,16,128]{2,1,0:T(8,128)S(1)}, u32[]{:S(2)}, u32[]{:S(2)}) %all-to-all-start.4) | async-done | bytes 65568 | tf_op jit(solution)/shard_map/all_to_all | solution.py:289
  78.7 0.6 reduce_sum.29
  (3 shorter events, 0.0 us)
Async XLA Ops:
  3.6 5.0 %copy-start.2 = (s32[128,4,64]{0,2,1:T(8,128)S(1)}, s32[128,4,64]{0,2,1:T(8,128)}, u32[]{:S(2)}) copy-start(s32[128,4,64]{0,2,1:T(8,128)} %param.15) | copy-start | bytes 393220
  3.6 5.0 %copy-start.3 = (s32[128,4]{0,1:T(4,128)S(1)}, s32[128,4]{0,1:T(4,128)}, u32[]{:S(2)}) copy-start(s32[128,4]{0,1:T(4,128)} %param.14) | copy-start | bytes 6148
  3.6 14.7 %all-to-all-start = ((bf16[4,4,64,512]{3,2,1,0:T(8,128)(2,1)}), bf16[4,4,64,512]{3,2,1,0:T(8,128)(2,1)S(1)}, u32[]{:S(2)}, u32[]{:S(2)}) async-start(bf16[4,4,64,512]{3,2,1,0:T(8,128)(2,1)} %get-tuple-element.19), calls=%async_computation | async-start | bytes 2097152 | tf_op jit(solution)/shard_map/all_to_all | solution.py:259
  19.7 7.5 %all-to-all-start.1 = ((f32[4,8,256]{2,1,0:T(8,128)}), f32[4,8,256]{2,1,0:T(8,128)S(1)}, u32[]{:S(2)}, u32[]{:S(2)}) async-start(f32[4,8,256]{2,1,0:T(8,128)} %get-tuple-element.32), calls=%async_computation.1 | async-start | bytes 65536 | tf_op jit(solution)/shard_map/all_to_all | solution.py:273
  24.7 46.8 %copy-start = (bf16[256,2048]{1,0:T(8,128)(2,1)S(1)}, bf16[256,2048]{1,0:T(8,128)(2,1)}, u32[]{:S(2)}) copy-start(bf16[256,2048]{1,0:T(8,128)(2,1)} %refs_4_.1) | copy-start | bytes 3145732
  28.1 23.2 %all-to-all-start.2 = ((f32[8,16,128]{2,1,0:T(8,128)}), f32[8,16,128]{2,1,0:T(8,128)S(1)}, u32[]{:S(2)}, u32[]{:S(2)}) async-start(f32[8,16,128]{2,1,0:T(8,128)} %shard_map.124), calls=%async_computation.2 | async-start | bytes 131072 | tf_op jit(solution)/shard_map/all_to_all | solution.py:286
  42.6 28.9 %collective-permute-start = (bf16[4,64,512]{2,1,0:T(8,128)(2,1)}, bf16[4,64,512]{2,1,0:T(8,128)(2,1)S(1)}, u32[]{:S(2)}, u32[]{:S(2)}) collective-permute-start(bf16[4,64,512]{2,1,0:T(8,128)(2,1)} %get-tuple-element.23), channel_id=1, source_target_pairs={{0,1},{1,2},{2,3},{3,0},{4,5},{5,6},{6,7},{7,4},{8,9},{9,10},{10,1... | collective-permute-start | bytes 786440 | tf_op jit(solution)/shard_map/ppermute | solution.py:257
  44.8 26.7 %collective-permute-start.1 = (bf16[4,64,512]{2,1,0:T(8,128)(2,1)}, bf16[4,64,512]{2,1,0:T(8,128)(2,1)S(1)}, u32[]{:S(2)}, u32[]{:S(2)}) collective-permute-start(bf16[4,64,512]{2,1,0:T(8,128)(2,1)} %get-tuple-element.24), channel_id=1, source_target_pairs={{0,2},{1,3},{2,0},{3,1},{4,6},{5,7},{6,4},{7,5},{8,10},{9,11},{10,... | collective-permute-start | bytes 786440 | tf_op jit(solution)/shard_map/ppermute | solution.py:257
  48.5 23.0 %copy-start.1 = (bf16[4,64,512]{2,1,0:T(8,128)(2,1)S(1)}, bf16[4,64,512]{2,1,0:T(8,128)(2,1)}, u32[]{:S(2)}) copy-start(bf16[4,64,512]{2,1,0:T(8,128)(2,1)} %get-tuple-element.22.refs_0_.after) | copy-start | bytes 786436
  48.5 23.0 %collective-permute-start.2 = (bf16[4,64,512]{2,1,0:T(8,128)(2,1)}, bf16[4,64,512]{2,1,0:T(8,128)(2,1)S(1)}, u32[]{:S(2)}, u32[]{:S(2)}) collective-permute-start(bf16[4,64,512]{2,1,0:T(8,128)(2,1)} %get-tuple-element.25), channel_id=1, source_target_pairs={{0,3},{1,0},{2,1},{3,2},{4,7},{5,4},{6,5},{7,6},{8,11},{9,8},{10,9... | collective-permute-start | bytes 786440 | tf_op jit(solution)/shard_map/ppermute | solution.py:257
  64.7 14.1 %all-to-all-start.4 = ((f32[8,16,128]{2,1,0:T(8,128)}), f32[8,16,128]{2,1,0:T(8,128)S(1)}, u32[]{:S(2)}, u32[]{:S(2)}) async-start(f32[8,16,128]{2,1,0:T(8,128)} %broadcast_in_dim.5), calls=%async_computation.4 | async-start | bytes 131072 | tf_op jit(solution)/shard_map/all_to_all | solution.py:289
